TPU v7x, 32 devices: a whole 2x2x4 slice. The times are simulated.
32 devices in a mesh: elem: 8 (over z, y), snap: 4 (over x, core).
Axes of the slice: x: 2, y: 2, z: 4, core: 2. Of those that a mesh axis runs over, the one named last changes fastest.
Arguments:
- node_basis: bfloat16 [8192, 1536], P('elem'), may hold values from -0.25 to 0.25
- stiff_terms: bfloat16 [16, 24, 24], replicated, may hold values from -1.25 to 1.25
- reduced_coords: bfloat16 [512, 32], P(None, 'snap'), may hold values from -6 to 6
- sample_list: int32 [64], replicated, may hold values from 0 to 255, as said below
- connectivity: int32 [256, 8], replicated, may hold values from -1 to 8191, as said below
- node_slot: int32 [8192], replicated, may hold values from 0 to 8191, as said below
- elem_device: int32 [64], replicated, may hold values from 0 to 7, as said below
Outputs:
- ortho_panel: float32 [128, 512, 512], P('elem', 'snap')
- triangle_factor: float32 [512, 512], P('elem')
Inputs may be any that keep to these rules, and one draw needn't show every extreme that they name: `sample_list`: distinct element ids. `connectivity`: each element lists 4, 6 or 8 live nodes first and -1 after them; the live nodes of one element are owned by distinct indices of elem (owner = node_slot // 1024); for every index d of elem and every owner o, at most 16 sampled elements computed on d have a live node owned by o, and some pair (d, o) reaches 16. `node_slot`: a permutation. `elem_device`: each index of elem computes at most 16 sampled elements; some index computes exactly 16.
All inputs are finite; a program needn't handle non-finite values.
Results may differ from a plain program's by a relative error of at most 0.0056.
Values may be sent and summed in bfloat16 or wider, within the bound.
No kernel may reach another device: no remote copies, remote signals or barrier semaphores. Data moves between devices by JAX's collectives and lax.ppermute only.
A program may use at most 64 MiB of HBM per device.

v0:
```python
import jax
import jax.numpy as jnp
from jax import lax
from jax.sharding import PartitionSpec as P

MODES = 512
ENODES = 8
NDOF = 3


def shards(
    node_basis, stiff_terms, reduced_coords, sample_list, connectivity, node_slot, elem_device
):
    devices = lax.axis_size("elem")
    groups = lax.axis_size("snap")
    elem_rank = lax.axis_index("elem")
    snap_rank = lax.axis_index("snap")
    node_rows = node_basis.shape[0]
    sampled = sample_list.shape[0]
    capacity = 2 * sampled // devices
    pair_bound = (capacity * ENODES + devices - 1) // devices
    node_ids = connectivity[sample_list]
    live_nodes = node_ids >= 0
    stored_rows = jnp.where(live_nodes, node_slot[jnp.maximum(node_ids, 0)], 0)
    owners = stored_rows // node_rows
    local_rows = stored_rows % node_rows
    position_ids = jnp.arange(sampled, dtype=jnp.int32)
    earlier = position_ids[None, :] < position_ids[:, None]
    same_device = elem_device[None, :] == elem_device[:, None]
    in_group = earlier & same_device
    slot_ids = jnp.sum(in_group.astype(jnp.int32), axis=1)
    owner_ids = jnp.arange(devices, dtype=jnp.int32)
    owned_mask = jnp.any(live_nodes[:, :, None] & (owners[:, :, None] == owner_ids), axis=1).astype(
        jnp.float32
    )
    ranks_by_owner = jnp.dot(
        in_group.astype(jnp.float32), owned_mask, precision=lax.Precision.HIGHEST
    ).astype(jnp.int32)
    peer_ranks = jnp.take_along_axis(ranks_by_owner, owners, axis=1)
    sending = live_nodes & (owners == elem_rank)
    target = jnp.where(sending, elem_device[:, None], devices)
    row_table = (
        jnp.full((devices, pair_bound), -1, jnp.int32)
        .at[target, peer_ranks]
        .set(local_rows, mode="drop")
    )
    send_rows = node_basis[jnp.maximum(row_table, 0)]
    outgoing = jnp.where((row_table >= 0)[:, :, None], send_rows, jnp.zeros((), jnp.bfloat16))
    incoming = lax.all_to_all(outgoing, "elem", split_axis=0, concat_axis=0, tiled=True)
    at_device = elem_device == elem_rank
    slot_index = jnp.where(at_device, slot_ids, capacity)
    slot_elem = (
        jnp.full((capacity,), sampled, jnp.int32).at[slot_index].set(position_ids, mode="drop")
    )
    slot_live = slot_elem < sampled
    picked = jnp.minimum(slot_elem, sampled - 1)
    slot_rows = incoming[owners[picked], jnp.minimum(peer_ranks[picked], pair_bound - 1)]
    slot_mask = live_nodes[picked] & slot_live[:, None]
    local_basis = jnp.where(slot_mask[:, :, None], slot_rows, jnp.zeros((), jnp.bfloat16))
    element_basis = local_basis.reshape(capacity, ENODES * NDOF, MODES)
    coords_all = lax.all_gather(reduced_coords, "snap", axis=1, tiled=True)
    displaced = jnp.einsum(
        "ekm,ms->eks", element_basis, coords_all, preferred_element_type=jnp.float32
    ).astype(jnp.bfloat16)
    forces = jnp.einsum(
        "tkl,els->ekst", stiff_terms, displaced, preferred_element_type=jnp.float32
    ).astype(jnp.bfloat16)
    forces = forces.reshape(capacity, ENODES * NDOF, -1)
    band_width = MODES // groups
    band_basis = lax.dynamic_slice_in_dim(element_basis, snap_rank * band_width, band_width, 2)
    banded = jnp.einsum(
        "ekm,ekc->emc", band_basis, forces, preferred_element_type=jnp.float32
    ).astype(jnp.bfloat16)
    band_rows = banded.reshape(-1, banded.shape[2])
    columns = band_rows.shape[1]
    total_rows = sampled * MODES
    partial_gram = lax.dot_general(
        band_rows, band_rows, (((0,), (0,)), ((), ())), preferred_element_type=jnp.float32
    )
    gram_matrix = lax.psum(partial_gram, ("elem", "snap"))
    gram_matrix = gram_matrix / total_rows
    lower_factor = jnp.linalg.cholesky(gram_matrix)
    identity_matrix = jnp.eye(columns, dtype=jnp.float32)
    lower_inverse = jax.scipy.linalg.solve_triangular(lower_factor, identity_matrix, lower=True)
    ortho_rows = lax.dot_general(
        band_rows.astype(jnp.float32),
        lower_inverse,
        (((1,), (1,)), ((), ())),
        precision=lax.Precision.HIGHEST,
        preferred_element_type=jnp.float32,
    )
    share = columns // devices
    upper_rows = lax.dynamic_slice_in_dim(lower_factor.T, elem_rank * share, share, 0)
    return (ortho_rows.reshape(banded.shape), upper_rows)


def solution(mesh):
    placed = (P("elem", None), P(), P(None, "snap"), P(), P(), P(), P())
    return jax.shard_map(
        shards,
        mesh=mesh,
        in_specs=placed,
        out_specs=(P("elem", "snap", None), P("elem", None)),
        check_vma=False,
    )
```

profile of v0, /device:TPU:0, one launch (start us, length us, event | category | flops | bytes accessed | tf_op | source)
XLA Modules:
  0.0 404.8 jit_solution(5960477116996220832)
XLA Ops:
  8.2 1.2 compare_select_fusion.7
  11.0 3.1 gather_fusion.2
  15.3 2.6 gather_fusion.7
  18.3 22.1 %scatter_fusion = s32[8,16]{1,0:T(8,128)S(1)} fusion(s32[8,16]{1,0:T(8,128)S(1)} %broadcast_in_dim.96, s32[512]{0:T(512)S(1)} %reshape.365, s32[512]{0:T(512)S(1)} %reshape.367), kind=kCustom, calls=%fused_computation.9 | custom fusion | bytes 10240 | tf_op jit(solution)/shard_map/scatter | solution.py:45
  41.9 1.5 broadcast_select_fusion
  43.5 7.3 %all-to-all-start = ((bf16[8,16,1536]{2,1,0:T(8,128)(2,1)}), bf16[8,16,1536]{2,1,0:T(8,128)(2,1)S(1)}, u32[]{:S(2)}, u32[]{:S(2)}) async-start(bf16[8,16,1536]{2,1,0:T(8,128)(2,1)} %broadcast_select_fusion), calls=%async_computation | async-start | bytes 786432 | tf_op jit(solution)/shard_map/all_to_all | solution.py:49
  54.1 1.4 gather_fusion.4
  57.8 1.4 and_select_fusion
  59.2 1.4 gather_fusion.5
  60.9 6.6 %all_gather.3 = bf16[512,32]{0,1:T(8,128)(2,1)} all-gather(bf16[512,8]{0,1:T(8,128)(2,1)} %param.9), channel_id=1, replica_groups=mesh['elem'=8,'snap'=4] {'snap'}, dimensions={1}, use_global_device_ids=true | all-gather | bytes 40960 | tf_op jit(solution)/shard_map/all_gather | solution.py:61
  67.5 2.8 gather_fusion.6
  70.3 1.9 gather.47
  72.2 1.1 broadcast_select_fusion.1
  73.3 2.9 fusion
  76.2 4.2 %copy.58 = bf16[16,24,32,16]{3,2,1,0:T(8,128)(2,1)} copy(bf16[16,24,32,16]{2,1,3,0:T(8,128)(2,1)} %fusion) | data formatting | bytes 786432 | tf_op jit(solution)/shard_map/convert_element_type | solution.py:67
  80.4 6.9 %reshape.277 = bf16[16,24,512]{2,1,0:T(8,128)(2,1)} reshape(bf16[16,24,32,16]{3,2,1,0:T(8,128)(2,1)} %copy.58) | data formatting | bytes 786432 | tf_op jit(solution)/shard_map/reshape | solution.py:68
  87.3 1.8 convolution_convert_fusion
  89.1 1.3 copy-done.2
  90.4 2.3 convolution_bitcast_fusion
  93.5 1.1 fusion.19
  94.6 128.7 %all-reduce.3.cloned.1.call-done = f32[512,512]{0,1:T(8,128)} async-done(((f32[512,512]{0,1:T(8,128)}), f32[512,512]{0,1:T(8,128)}) %all-reduce.3.cloned.1.call-update) | async-done | bytes 1048592 | tf_op jit(solution)/shard_map/psum | solution.py:80
  223.3 2.3 broadcast_multiply_fusion
  225.6 2.5 copy.61
  228.2 1.8 fusion.9
  231.0 11.7 %cholesky.104 = f32[128,128]{1,0:T(8,128)S(1)} custom-call(f32[128,128]{1,0:T(8,128)S(1)} %cholesky.266), custom_call_target="Cholesky" | custom-call | tf_op jit(solution)/shard_map/jit(cholesky)/cholesky | solution.py:82
  243.3 9.8 %custom-call.31 = f32[1,128,128]{1,2,0:T(8,128)S(1)} custom-call(f32[1,128,128]{2,1,0:T(8,128)S(1)} %get-tuple-element.41), custom_call_target="InvertDiagBlocksLowerTriangular" | custom-call | tf_op jit(solution)/shard_map/jit(cholesky)/cholesky | solution.py:82
  253.1 1.3 fusion.25
  254.5 2.1 convolution_subtract_fusion.3
  258.3 11.9 %cholesky.217 = f32[128,128]{1,0:T(8,128)S(1)} custom-call(f32[128,128]{1,0:T(8,128)S(1)} %cholesky.270), custom_call_target="Cholesky" | custom-call | tf_op jit(solution)/shard_map/jit(cholesky)/cholesky | solution.py:82
  270.2 2.0 cholesky.224
  274.1 9.8 %custom-call.32 = f32[1,128,128]{1,2,0:T(8,128)S(1)} custom-call(f32[1,128,128]{2,1,0:T(8,128)S(1)} %get-tuple-element.38), custom_call_target="InvertDiagBlocksLowerTriangular" | custom-call | tf_op jit(solution)/shard_map/jit(cholesky)/cholesky | solution.py:82
  283.9 1.8 convolution_dynamic-update-slice_fusion
  285.8 1.4 convolution_subtract_fusion.4
  287.2 11.7 %cholesky.238 = f32[128,128]{1,0:T(8,128)S(1)} custom-call(f32[128,128]{1,0:T(8,128)S(1)} %cholesky.275), custom_call_target="Cholesky" | custom-call | tf_op jit(solution)/shard_map/jit(cholesky)/cholesky | solution.py:82
  300.2 9.8 %custom-call.33 = f32[1,128,128]{1,2,0:T(8,128)S(1)} custom-call(f32[1,128,128]{2,1,0:T(8,128)S(1)} %get-tuple-element.35), custom_call_target="InvertDiagBlocksLowerTriangular" | custom-call | tf_op jit(solution)/shard_map/jit(cholesky)/cholesky | solution.py:82
  310.8 1.4 convolution_subtract_fusion.5
  312.2 11.9 %cholesky.255 = f32[128,128]{1,0:T(8,128)S(1)} custom-call(f32[128,128]{1,0:T(8,128)S(1)} %convolution_subtract_fusion.5), custom_call_target="Cholesky" | custom-call | tf_op jit(solution)/shard_map/jit(cholesky)/cholesky | solution.py:82
  327.9 2.5 fusion.10
  331.4 13.8 %while.1 = (s32[]{:T(128)}, f32[512,512]{1,0:T(8,128)}, s32[4,2]{0,1:T(2,128)S(1)}, f32[4,128,128]{2,1,0:T(8,128)}, s32[]{:T(128)}) while((s32[]{:T(128)}, f32[512,512]{1,0:T(8,128)}, s32[4,2]{0,1:T(2,128)S(1)}, f32[4,128,128]{2,1,0:T(8,128)}, s32[]{:T(128)}) %tuple.36), condition=%wide.while_cond, body=%wide.while_body.sunk | while | flops 2 | bytes 132205 | solution.py:84
  332.0 2.8 bitcast_dynamic-update-slice_fusion.2
  335.4 2.8 bitcast_dynamic-update-slice_fusion.2
  338.9 2.8 bitcast_dynamic-update-slice_fusion.2
  342.4 2.8 bitcast_dynamic-update-slice_fusion.2
  345.1 40.1 %custom-call.34 = f32[4,128,128]{1,2,0:T(8,128)S(1)} custom-call(f32[4,128,128]{2,1,0:T(8,128)} %get-tuple-element.9), custom_call_target="InvertDiagBlocksLowerTriangular" | custom-call | tf_op jit(solution)/shard_map/jit(_solve_triangular)/triangular_solve | solution.py:84
  386.4 1.4 convolution_subtract_fusion.1
  388.2 1.6 convolution_subtract_fusion
  390.2 1.7 convolution_subtract_fusion.2
  392.4 5.1 %fusion.2 = f32[16,128,512]{2,1,0:T(8,128)} fusion(bf16[16,128,512]{2,1,0:T(8,128)(2,1)S(1)} %copy-done.3, f32[128,512]{1,0:T(8,128)S(1)} %fusion.32, f32[128,512]{1,0:T(8,128)S(1)} %fusion.33, f32[128,512]{1,0:T(8,128)S(1)} %fusion.35, f32[128,512]{1,0:T(8,128)S(1)} %fusion.21), kind=kOutput, calls=%fused_computation.28 | convolution fusion | flops 6443237376 | bytes 7340032 | tf_op jit(solution)/shard_map/dot_general | solution.py:85
  (96 shorter events, 26.7 us)
Async XLA Ops:
  7.2 33.9 %copy-start = (bf16[1024,1536]{1,0:T(8,128)(2,1)S(1)}, bf16[1024,1536]{1,0:T(8,128)(2,1)}, u32[]{:S(2)}) copy-start(bf16[1024,1536]{1,0:T(8,128)(2,1)} %param.7) | copy-start | bytes 9437188
  7.2 3.8 copy-start.1
  10.9 4.0 copy-start.8
  14.3 0.6 copy-start.5
  43.5 24.0 %all-to-all-start = ((bf16[8,16,1536]{2,1,0:T(8,128)(2,1)}), bf16[8,16,1536]{2,1,0:T(8,128)(2,1)S(1)}, u32[]{:S(2)}, u32[]{:S(2)}) async-start(bf16[8,16,1536]{2,1,0:T(8,128)(2,1)} %broadcast_select_fusion), calls=%async_computation | async-start | bytes 786432 | tf_op jit(solution)/shard_map/all_to_all | solution.py:49
  50.7 172.6 %all-reduce.3.cloned.1.call-start = ((), (), s32[]{:S(2)}) async-start(), calls=%async_computation.1 | async-start | bytes 2097152 | tf_op jit(solution)/shard_map/psum | solution.py:80
  67.5 4.7 %copy-start.7 = (pred[16,24]{1,0:T(8,128)(4,1)S(1)}, pred[16,24]{1,0:T(8,128)(4,1)}, u32[]{:S(2)}) copy-start(pred[16,24]{1,0:T(8,128)(4,1)} %copy.52) | copy-start | bytes 1156
  89.1 1.3 copy-start.2
  229.9 1.0 copy-start.4
  242.7 0.6 copy-start.6
  387.7 4.6 %copy-start.3 = (bf16[16,128,512]{2,1,0:T(8,128)(2,1)S(1)}, bf16[16,128,512]{2,1,0:T(8,128)(2,1)}, u32[]{:S(2)}) copy-start(bf16[16,128,512]{2,1,0:T(8,128)(2,1)} %copy-done.2) | copy-start | bytes 6291460
Sparse Core Ops, SparseCore 0:
  92.9 130.4 all-reduce.2
where the time goes:
time: 412 us; the launch traced here: 405 us
  other arithmetic  139 us (34%)
  waiting for transfers between devices  129 us (31%)
  local copies, waits for them, and re-layouts  77.8 us (19%)
  matrix products  28.2 us (7%)
  between operations  17.3 us (4%)
  starting transfers between devices  7.3 us (2%)
  blocking collectives  6.59 us (2%)
    psum x1, waiting for transfers between devices, shards(): gram_matrix = lax.psum(partial_gram, ('elem', 'snap'))  129 us
    another operation x15, other arithmetic, shards(): lower_factor = jnp.linalg.cholesky(gram_matrix)  81.3 us
    another operation x3, other arithmetic, shards(): jax.scipy.linalg.solve_triangular(lower_factor, identity_matrix, lower=True)  42.7 us
    scatter x1, local copies, waits for them, and re-layouts, shards(): row_table = jnp.full((devices, pair_bound), -1, jnp.int32).at[target, pee...  22.1 us
    another operation x12, local copies, waits for them, and re-layouts  13.8 us
    another operation x6, matrix products, shards(): lower_factor = jnp.linalg.cholesky(gram_matrix)  8.94 us
  transfers between devices with their start and end apart: 2, of which 1 were waited for; matrix products, arithmetic and copies ran while one was open for 3% of the time, Pallas kernels for 0%

commit v1 on v0

v1 whole, which is shorter than its diff:
```python
import functools

import jax
import jax.numpy as jnp
from jax import lax
from jax.experimental import pallas as pl
from jax.experimental.pallas import tpu as pltpu
from jax.sharding import PartitionSpec as P

F32, BF16, I32 = jnp.float32, jnp.bfloat16, jnp.int32
NT = (((1,), (1,)), ((), ()))
NN = (((1,), (0,)), ((), ()))
LANES = 128
TILE = 256
BLOCK = 128
STEP = 8
VMEM_BYTES = 60 * 1024 * 1024
JOINED_LIMIT = 1 << 22


def dot(a, b, dims=NN):
    return lax.dot_general(a, b, dims, preferred_element_type=F32)


def split(x):
    high = x.astype(BF16)
    return high, (x - high.astype(F32)).astype(BF16)


def dot3(a, b, dims=NN):
    (ah, al), (bh, bl) = a, b
    return dot(ah, bh, dims) + (dot(ah, bl, dims) + dot(al, bh, dims))


def iota(shape, dim):
    return lax.broadcasted_iota(I32, shape, dim)


def quotient(x, n):
    return jnp.floor((x.astype(F32) + 0.5) * (1.0 / n)).astype(I32)


def node_places(sample, links, table):
    positions, elems = links.shape
    sampled = sample.shape[1]
    pick = (iota((elems, sampled), 0) == sample).astype(F32).astype(BF16)
    shifted = links + 1
    parts = jnp.concatenate([(shifted >> 8).astype(F32), (shifted & 255).astype(F32)], axis=0)
    found = dot(parts.astype(BF16), pick)
    nodes = (found[:positions] * 256.0 + found[positions:]).astype(I32) - 1
    halves = jnp.concatenate([(table >> 8).astype(F32), (table & 255).astype(F32)], axis=1).T.astype(BF16)
    high, low = jnp.maximum(nodes, 0) >> 7, jnp.maximum(nodes, 0) & (LANES - 1)
    places = jnp.zeros((positions, sampled), F32)
    for p in range(positions):
        rows = (iota((table.shape[0], sampled), 0) == high[p : p + 1]).astype(F32).astype(BF16)
        both = dot(halves, rows)
        here = iota((LANES, sampled), 0) == low[p : p + 1]
        value = both[:LANES] * 256.0 + both[LANES:]
        value = jnp.sum(jnp.where(here, value, 0.0), axis=0, keepdims=True)
        places = jnp.where(iota((positions, sampled), 0) == p, value, places)
    return jnp.where(nodes >= 0, places, -1.0)


def slot_picks(elem_device, device, capacity):
    sampled = elem_device.shape[1]
    mine = (elem_device == device).astype(F32)
    before = (iota((sampled, sampled), 0) < iota((sampled, sampled), 1)).astype(F32).astype(BF16)
    ranks = dot(jnp.broadcast_to(mine, (16, sampled)).astype(BF16), before)[0:1]
    return jnp.where(iota((capacity, sampled), 0).astype(F32) == ranks, mine, 0.0)


def owner_kernel(
    devices, groups, capacity, ndof, ids, sample, links, table, elem_device, basis, shared, slots, owners
):
    elem_rank, snap_rank = ids[0], ids[1]
    node_rows, width = basis.shape
    modes = width // ndof
    band = modes // groups
    sampled = sample.shape[1]
    quarter = sampled // groups
    first = slots.shape[1] - capacity
    places = node_places(sample[...], links[...], table[...])
    owner = jnp.floor((places + 0.5) * (1.0 / node_rows))
    owners[...] = jnp.where(places >= 0, owner, -1.0)
    here = (places >= 0) & (owner == elem_rank.astype(F32))
    local = places - (elem_rank * node_rows).astype(F32) + 1.0
    local = jnp.sum(jnp.where(here, local, 0.0), axis=0, keepdims=True)
    wanted = (iota((quarter, sampled), 1) == iota((quarter, sampled), 0) + snap_rank * quarter).astype(F32)
    picks = [wanted] + [slot_picks(elem_device[...], d, capacity) for d in range(devices)]
    row = jnp.sum(jnp.concatenate(picks, axis=0) * local, axis=1, keepdims=True).astype(I32) - 1
    one_hot = (iota((row.shape[0], node_rows), 1) == row).astype(F32).astype(BF16)
    for c in range(ndof):
        rows = dot(one_hot, basis[:, c * modes : (c + 1) * modes])
        full = rows[:quarter].astype(BF16)
        part = jnp.zeros((devices * capacity, band), F32)
        for k in range(groups):
            part = jnp.where(snap_rank == k, rows[quarter:, k * band : (k + 1) * band], part)
        part = part.astype(BF16)
        for d in range(shared.shape[0]):
            shared[d, c * quarter : (c + 1) * quarter, :] = full
        for d in range(devices):
            slots[d, first:, c * band : (c + 1) * band] = part[d * capacity : (d + 1) * capacity]
    for d in range(devices):
        slots[d, first:, ndof * band :] = jnp.zeros((capacity, modes - ndof * band), BF16)


def owner_kernel_joined(devices, groups, capacity, ndof, *refs):
    owner_kernel(devices, groups, capacity, ndof, *refs[:-2], refs[-2], refs[-2], refs[-1])


def place_one_hot(owner_col, lane_count, ndof, pitch, live, members):
    rows = owner_col.shape[0]
    index = iota((rows, 1), 0)
    member, row = index // pitch, index % pitch
    position = quotient(row, ndof)
    dof = row - position * ndof
    target = (owner_col.astype(I32) * ndof + dof) * members + member
    target = jnp.where((owner_col >= 0) & (row < live), target, -1)
    return (iota((rows, lane_count), 1) == target).astype(F32).astype(BF16)


def owner_rows(owners, rows, ndof, pitch):
    positions = owners.shape[0]
    position = quotient(iota((rows, positions), 0) % pitch, ndof)
    pick = (position == iota((rows, positions), 1)).astype(F32).astype(BF16)
    return dot(pick, owners.astype(BF16))


def element_kernel(ndof, pitch, ids, got, coords, owners, out):
    snap_rank = ids[1]
    devices, _, modes = got.shape
    positions, sampled = owners.shape
    members = 16
    live = positions * ndof
    quarter = out.shape[1] // pitch
    snaps = out.shape[0] - 2 * pitch
    per_tile = TILE // pitch
    rows = members * pitch
    own = owner_rows(owners[...], rows, ndof, pitch)
    for h in range(quarter // members):
        first = snap_rank * quarter + h * members
        at = iota((rows, sampled), 1) == iota((rows, sampled), 0) // pitch + first
        owner_col = jnp.sum(jnp.where(at, own, 0.0), axis=1, keepdims=True)
        source = jnp.concatenate(
            [
                got[o, c * quarter + h * members : c * quarter + (h + 1) * members, :]
                for o in range(devices)
                for c in range(ndof)
            ],
            axis=0,
        )
        basis = dot(place_one_hot(owner_col, source.shape[0], ndof, pitch, live, members), source).astype(BF16)
        moved = dot(coords[...], basis, NT).astype(BF16)
        out[0:snaps, h * rows : (h + 1) * rows] = moved
        for g in range(rows // TILE):
            part = basis[g * TILE : (g + 1) * TILE]
            square = dot(part, part, NT)
            block = jnp.zeros((pitch, TILE), F32)
            for i in range(per_tile):
                inside = iota((pitch, TILE), 1) // pitch == i
                block = jnp.where(inside, square[i * pitch : (i + 1) * pitch], block)
            high, low = split(block)
            lanes = slice(h * rows + g * TILE, h * rows + (g + 1) * TILE)
            out[snaps : snaps + pitch, lanes] = high
            out[snaps + pitch :, lanes] = low


def spread(x):
    return jnp.broadcast_to(x, (STEP, LANES))


def factor_block(block):
    count = BLOCK // STEP
    left = [block[STEP * c : STEP * c + STEP] for c in range(count)]
    right = [
        (iota((STEP, LANES), 1) == iota((STEP, LANES), 0) + STEP * c).astype(F32)
        for c in range(count)
    ]
    sub = iota((STEP, LANES), 0)
    upper, inverse = [], []
    for j in range(count):
        base = STEP * j
        s = {
            (i, k): spread(left[j][i : i + 1, base + k : base + k + 1])
            for k in range(STEP)
            for i in range(k, STEP)
        }
        ul = [spread(left[j][k : k + 1]) for k in range(STEP)]
        ur = [spread(right[j][k : k + 1]) for k in range(STEP)]
        scale, low = [], {}
        out_l, out_r = jnp.zeros((STEP, LANES), F32), jnp.zeros((STEP, LANES), F32)
        for k in range(STEP):
            root = lax.rsqrt(s[k, k])
            scale.append(root)
            for i in range(k + 1, STEP):
                low[i, k] = s[i, k] * root
            for m in range(k + 1, STEP):
                for i in range(m, STEP):
                    s[i, m] = s[i, m] - low[i, k] * low[m, k]
            ul[k], ur[k] = ul[k] * root, ur[k] * root
            for i in range(k + 1, STEP):
                ul[i] = ul[i] - low[i, k] * ul[k]
                ur[i] = ur[i] - low[i, k] * ur[k]
            out_l = jnp.where(sub == k, ul[k], out_l)
            out_r = jnp.where(sub == k, ur[k], out_r)
        keep = iota((STEP, LANES), 1) >= sub + base
        upper.append(jnp.where(keep, out_l, 0.0))
        inverse.append(out_r)
        for c in range(j + 1, count):
            column = [spread(left[c][:, base + k : base + k + 1]) for k in range(STEP)]
            for k in range(STEP):
                m = column[k] * scale[k]
                for i in range(k + 1, STEP):
                    column[i] = column[i] - m * low[i, k]
                left[c] = left[c] - m * ul[k]
                right[c] = right[c] - m * ur[k]
    return jnp.concatenate(upper, axis=0), jnp.concatenate(inverse, axis=0)


def panel_kernel(
    ndof, pitch, total_rows, ids, every, got, owners, elem_device, stiff, panel, factor, forces, halves, work, upper
):
    elem_rank = ids[0]
    groups, height, lanes = every.shape
    snaps = height - 2 * pitch
    terms, live, _ = stiff.shape
    columns = snaps * terms
    capacity, band, _ = panel.shape
    devices = got.shape[0]
    positions, sampled = owners.shape
    per_tile = TILE // pitch
    tiles = [(q, t) for q in range(groups) for t in range(lanes // TILE)]
    slot_rows = capacity * pitch
    slot_tiles = slot_rows // TILE
    chunk = 8

    picks = slot_picks(elem_device[...], elem_rank, capacity)
    member = iota((slot_rows, capacity), 0) // pitch
    expand = (member == iota((slot_rows, capacity), 1)).astype(F32).astype(BF16)
    picks = dot(expand, picks.astype(BF16))
    own = owner_rows(owners[...], slot_rows, ndof, pitch)
    owner_col = jnp.sum(picks * (own + 1.0), axis=1, keepdims=True) - 1.0
    which = jnp.sum(picks * (iota((slot_rows, sampled), 1) + 1).astype(F32), axis=1, keepdims=True).astype(I32) - 1
    first = got.shape[1] - capacity
    source = jnp.concatenate(
        [got[o, first:, c * band : (c + 1) * band] for o in range(devices) for c in range(ndof)], axis=0
    )
    basis = dot(place_one_hot(owner_col, source.shape[0], ndof, pitch, live, capacity), source)
    basis_t = basis.T

    lane = which * pitch + iota((slot_rows, 1), 0) % pitch
    lane = jnp.where(which >= 0, lane, -1)
    slot_moved = jnp.zeros((snaps, slot_rows), F32)
    for n, (q, t) in enumerate(tiles):
        pick = (iota((slot_rows, TILE), 1) + n * TILE == lane).astype(F32).astype(BF16)
        slot_moved = slot_moved + dot(every[q, 0:snaps, t * TILE : (t + 1) * TILE], pick, NT)
    slot_moved = slot_moved.astype(BF16)

    tile_of = (iota((live, TILE), 1) % pitch == iota((live, TILE), 0)).astype(F32).astype(BF16)
    diagonal = iota((TILE, TILE), 0) // pitch == iota((TILE, TILE), 1) // pitch
    terms_wide = []
    for t in range(terms):
        wide = dot(stiff[t], tile_of)
        wide = jnp.concatenate([wide, jnp.zeros((pitch - live, TILE), F32)], axis=0)
        wide = jnp.concatenate([wide] * per_tile, axis=0)
        terms_wide.append(jnp.where(diagonal, wide, 0.0).astype(BF16))

    gram = None
    for start in range(0, len(tiles), chunk):
        part = tiles[start : start + chunk]
        moved = [every[q, 0:snaps, t * TILE : (t + 1) * TILE] for q, t in part]
        if start == 0:
            moved += [slot_moved[:, t * TILE : (t + 1) * TILE] for t in range(slot_tiles)]
        moved = jnp.concatenate(moved, axis=0)
        for t in range(terms):
            force = dot(moved, terms_wide[t], NT)
            for n in range(moved.shape[0] // snaps):
                for h in range(TILE // LANES):
                    piece = force[n * snaps : (n + 1) * snaps, h * LANES : (h + 1) * LANES]
                    forces[n * TILE // LANES + h, pl.ds(t, snaps, stride=terms), :] = piece
        if start == 0:
            for h in range(slot_rows // LANES):
                piece = forces[len(part) * TILE // LANES + h].astype(BF16).astype(F32)
                work[:, columns + h * LANES : columns + (h + 1) * LANES] = piece
        for n, (q, t) in enumerate(part):
            force = [forces[n * TILE // LANES + h] for h in range(TILE // LANES)]
            force = jnp.concatenate(force, axis=1).astype(BF16)
            cut = slice(t * TILE, (t + 1) * TILE)
            total = None
            for low in (0, 1):
                rows = every[q, snaps + low * pitch : snaps + (low + 1) * pitch, cut].astype(F32)
                wide = jnp.concatenate([rows] * per_tile, axis=0)
                term = dot(force, jnp.where(diagonal, wide, 0.0).astype(BF16))
                total = term if total is None else total + term
            halves[0, :, n * TILE : (n + 1) * TILE] = force
            halves[1, :, n * TILE : (n + 1) * TILE], halves[2, :, n * TILE : (n + 1) * TILE] = split(total)
        end = len(part) * TILE
        term = dot(halves[0, :, :end], halves[1, :, :end], NT) + dot(halves[0, :, :end], halves[2, :, :end], NT)
        gram = term if gram is None else gram + term
    work[:, :columns] = gram * (1.0 / total_rows)

    for b in range(columns // BLOCK):
        here = slice(b * BLOCK, (b + 1) * BLOCK)
        after = (b + 1) * BLOCK
        top, inverse = factor_block(work[here, here])
        upper[here, here] = top
        if b:
            upper[here, : b * BLOCK] = jnp.zeros((BLOCK, b * BLOCK), F32)
        inverse = split(inverse)
        across = dot3(inverse, split(work[here, after:]))
        work[here, after:] = across
        if after < columns:
            upper[here, after:] = across[:, : columns - after]
            down = dot3(split(work[after:columns, here]), inverse, NT)
            work[after:columns, after:] = work[after:columns, after:] - dot3(split(down), split(across))

    share = factor.shape[0]
    factor[...] = upper[pl.ds(pl.multiple_of(elem_rank * share, share), share), :]

    each = LANES // pitch
    for n in range(slot_rows // LANES):
        cut = slice(columns + n * LANES, columns + (n + 1) * LANES)
        high, low = split(work[:, cut])
        right = jnp.concatenate([high, low], axis=1)
        rows = basis_t[:, n * LANES : (n + 1) * LANES]
        left = jnp.concatenate(
            [jnp.where(iota((band, LANES), 1) // pitch == i, rows, 0.0) for i in range(each)], axis=0
        ).astype(BF16)
        result = dot(jnp.concatenate([left, left], axis=1), right, NT)
        for i in range(each):
            panel[n * each + i] = result[i * band : (i + 1) * band]


def shards(node_basis, stiff_terms, reduced_coords, sample_list, connectivity, node_slot, elem_device):
    devices = lax.axis_size("elem")
    groups = lax.axis_size("snap")
    node_rows, width = node_basis.shape
    modes, local_snaps = reduced_coords.shape
    snaps = local_snaps * groups
    ndof = width // modes
    terms, live, _ = stiff_terms.shape
    sampled = sample_list.shape[0]
    positions = connectivity.shape[1]
    capacity = 2 * sampled // devices
    quarter = sampled // groups
    pitch = 32
    band = modes // groups
    columns = snaps * terms
    total_rows = sampled * modes
    chunk_lanes = min(sampled * pitch, 8 * TILE)
    slot_rows = capacity * pitch

    ids = jnp.stack([lax.axis_index("elem"), lax.axis_index("snap")]).astype(I32)
    smem = pl.BlockSpec(memory_space=pltpu.SMEM)
    vmem = pl.BlockSpec(memory_space=pltpu.VMEM)
    params = pltpu.CompilerParams(vmem_limit_bytes=VMEM_BYTES)

    coords = lax.all_gather(reduced_coords.T, "snap", axis=0, tiled=True)
    sample_row = sample_list.reshape(1, sampled)
    device_row = elem_device.reshape(1, sampled)
    table = node_slot.reshape(-1, LANES)
    shared_rows = ndof * quarter
    joined = devices * (shared_rows + capacity) * modes <= JOINED_LIMIT
    if joined:
        sent = ((devices, shared_rows + capacity, modes),)
    else:
        sent = ((1, shared_rows, modes), (devices, capacity, modes))
    *sent, owners = pl.pallas_call(
        functools.partial(owner_kernel_joined if joined else owner_kernel, devices, groups, capacity, ndof),
        out_shape=tuple(jax.ShapeDtypeStruct(shape, BF16) for shape in sent)
        + (jax.ShapeDtypeStruct((positions, sampled), F32),),
        in_specs=[smem] + [vmem] * 5,
        out_specs=(vmem,) * (len(sent) + 1),
        compiler_params=params,
        name="owner_rows",
    )(ids, sample_row, connectivity.T, table, device_row, node_basis)
    slots = lax.all_to_all(sent[-1], "elem", split_axis=0, concat_axis=0, tiled=True)
    got = slots if joined else lax.all_gather(sent[0], "elem", axis=0, tiled=True)

    mine = pl.pallas_call(
        functools.partial(element_kernel, ndof, pitch),
        out_shape=jax.ShapeDtypeStruct((snaps + 2 * pitch, quarter * pitch), BF16),
        in_specs=[smem] + [vmem] * 3,
        out_specs=vmem,
        compiler_params=params,
        name="element_squares",
    )(ids, got, coords, owners)
    every = lax.all_gather(mine, "snap", axis=0)

    return pl.pallas_call(
        functools.partial(panel_kernel, ndof, pitch, total_rows),
        out_shape=(
            jax.ShapeDtypeStruct((capacity, band, columns), F32),
            jax.ShapeDtypeStruct((columns // devices, columns), F32),
        ),
        in_specs=[smem] + [vmem] * 5,
        out_specs=(vmem, vmem),
        scratch_shapes=[
            pltpu.VMEM(((chunk_lanes + slot_rows) // LANES, columns, LANES), F32),
            pltpu.VMEM((3, columns, chunk_lanes), BF16),
            pltpu.VMEM((columns, columns + slot_rows), F32),
            pltpu.VMEM((columns, columns), F32),
        ],
        compiler_params=params,
        name="panel",
    )(ids, every, slots, owners, device_row, stiff_terms)


def solution(mesh):
    placed = (P("elem", None), P(), P(None, "snap"), P(), P(), P(), P())
    return jax.shard_map(
        shards,
        mesh=mesh,
        in_specs=placed,
        out_specs=(P("elem", "snap", None), P("elem", None)),
        check_vma=False,
    )
```

time: 412 us -> 71.3 us (0.17); the launches traced: 405 us -> 71 us
  other arithmetic: 139 us -> 0.59 us
  waiting for transfers between devices: 129 us -> 8.84 us
  local copies, waits for them, and re-layouts: 77.8 us -> 0.8 us
  Pallas kernels: 0 us -> 39.4 us
  matrix products: 28.2 us -> 0 us
  between operations: 17.3 us -> 0.65 us
  blocking collectives: 6.59 us -> 13.4 us
    psum x1 -> x0, waiting for transfers between devices: 129 us -> none  [shards(): gram_matrix = lax.psum(partial_gram, ('elem', 'snap'))]
    another operation x18 -> x1, other arithmetic: 124 us -> 0.59 us  [shards(): jnp.stack([lax.axis_index('elem'), lax.axis_index('snap')]).astype(I32)]
    pallas_call x0 -> x3, Pallas kernels: none -> 39.4 us  [the longest x1 32.7 us: shards(): pl.pallas_call(functools.partial(panel_kernel, ndof, pitch, total_rows),...]
    scatter x2 -> x0, local copies, waits for them, and re-layouts: 23 us -> none  [the longest x1 22.1 us: shards(): row_table = jnp.full((devices, pair_bound), -1, jnp.int32).at[target, pee...]
    another operation x19 -> x0, local copies, waits for them, and re-layouts: 17.4 us -> none
    gather x17 -> x0, local copies, waits for them, and re-layouts: 16.8 us -> none  [the longest x2 4.7 us: shards(): incoming[owners[picked], jnp.minimum(peer_ranks[picked], pair_bound - 1)]]
    another operation x13 -> x0, matrix products: 16 us -> none  [the longest x6 8.94 us: shards(): lower_factor = jnp.linalg.cholesky(gram_matrix)]
    dot_general x5 -> x0, matrix products: 12.3 us -> none  [the longest x1 5.1 us: shards(): lax.dot_general(band_rows.astype(jnp.float32), lower_inverse, (((1,), (1,...]
  transfers between devices with their start and end apart: 2 -> 1, of which waited for: 1 -> 1; matrix products, arithmetic and copies ran while one was open for 3% -> 0% of each run, Pallas kernels for 0% -> 0%
where the time goes in v1:
time: 71.3 us; the launch traced here: 71 us
  Pallas kernels  39.4 us (55%)
  blocking collectives  13.4 us (19%)
  waiting for transfers between devices  8.84 us (12%)
  starting transfers between devices  7.28 us (10%)
  local copies, waits for them, and re-layouts  0.8 us (1%)
    pallas_call x1, Pallas kernels, shards(): pl.pallas_call(functools.partial(panel_kernel, ndof, pitch, total_rows),...  32.7 us
    all_to_all x1, waiting for transfers between devices, shards(): lax.all_to_all(sent[-1], 'elem', split_axis=0, concat_axis=0, tiled=True)  8.84 us
    all_gather x1, blocking collectives, shards(): every = lax.all_gather(mine, 'snap', axis=0)  7.79 us
    all_to_all x1, starting transfers between devices, shards(): lax.all_to_all(sent[-1], 'elem', split_axis=0, concat_axis=0, tiled=True)  7.28 us
    all_gather x1, blocking collectives, shards(): coords = lax.all_gather(reduced_coords.T, 'snap', axis=0, tiled=True)  5.64 us
    pallas_call x1, Pallas kernels, shards(): pl.pallas_call(functools.partial(owner_kernel_joined if joined else owner...  3.94 us
    pallas_call x1, Pallas kernels, shards(): pl.pallas_call(functools.partial(element_kernel, ndof, pitch), out_shape=...  2.75 us
  transfers between devices with their start and end apart: 1, of which 1 were waited for; matrix products, arithmetic and copies ran while one was open for 0% of the time, Pallas kernels for 0%

profile of v1, /device:TPU:0, one launch (start us, length us, event | category | flops | bytes accessed | tf_op | source)
XLA Modules:
  0.0 71.0 jit_solution(14155706329960330954)
XLA Ops:
  0.6 0.0 copy-start.1
  0.6 0.6 pad_add_fusion.refs_0_.ids
  1.2 3.9 %owner_rows.1 = (bf16[8,64,512]{2,1,0:T(8,128)(2,1)}, f32[8,64]{1,0:T(8,128)}) custom-call(s32[2]{0:T(128)} %pad_add_fusion.refs_0_.ids, s32[1,64]{1,0:T(1,128)} %bitcast.14, s32[8,256]{1,0:T(8,128)} %bitcast.10, s32[64,128]{1,0:T(8,128)} %bitcast.9, s32[1,64]{1,0:T(1,128)} %bitcast.12, bf16[1024,1536]{1,0:T(8,128)(2,1)} %refs_5_.1), custom_call_target="tpu_custom_call" | custom-call | tf_op jit(solution)/shard_map/owner_rows/pallas_call | solution.py:368
  5.2 7.3 %all-to-all-start = ((bf16[8,64,512]{2,1,0:T(8,128)(2,1)}), bf16[8,64,512]{2,1,0:T(8,128)(2,1)S(1)}, u32[]{:S(2)}, u32[]{:S(2)}) async-start(bf16[8,64,512]{2,1,0:T(8,128)(2,1)} %get-tuple-element.4), calls=%async_computation | async-start | bytes 1048576 | tf_op jit(solution)/shard_map/all_to_all | solution.py:377
  12.4 0.0 copy-done.1
  12.5 5.6 %all_gather.9.coords = bf16[32,512]{1,0:T(8,128)(2,1)} all-gather(bf16[8,512]{1,0:T(8,128)(2,1)S(1)} %bitcast.11), channel_id=1, replica_groups=mesh['elem'=8,'snap'=4] {'snap'}, dimensions={0}, use_global_device_ids=true | all-gather | bytes 40960 | tf_op jit(solution)/shard_map/all_gather | solution.py:358
  18.1 8.8 %all-to-all-done.got = bf16[8,64,512]{2,1,0:T(8,128)(2,1)S(1)} async-done(((bf16[8,64,512]{2,1,0:T(8,128)(2,1)}), bf16[8,64,512]{2,1,0:T(8,128)(2,1)S(1)}, u32[]{:S(2)}, u32[]{:S(2)}) %all-to-all-start) | async-done | bytes 524320 | tf_op jit(solution)/shard_map/all_to_all | solution.py:377
  26.9 0.0 copy-start
  26.9 0.8 %copy-done = bf16[8,64,512]{2,1,0:T(8,128)(2,1)} copy-done((bf16[8,64,512]{2,1,0:T(8,128)(2,1)}, bf16[8,64,512]{2,1,0:T(8,128)(2,1)S(1)}, u32[]{:S(2)}) %copy-start) | copy-done | bytes 524312
  27.7 2.8 %element_squares.1 = bf16[96,512]{1,0:T(8,128)(2,1)} custom-call(s32[2]{0:T(128)} %pad_add_fusion.refs_0_.ids, bf16[8,64,512]{2,1,0:T(8,128)(2,1)} %copy-done, bf16[32,512]{1,0:T(8,128)(2,1)} %all_gather.9.coords, f32[8,64]{1,0:T(8,128)} %get-tuple-element.5.owners), custom_call_target="tpu_custom_call" | custom-call | tf_op jit(solution)/shard_map/element_squares/pallas_call | solution.py:380
  30.5 7.8 %all-gather = bf16[384,512]{1,0:T(8,128)(2,1)} all-gather(bf16[96,512]{1,0:T(8,128)(2,1)} %element_squares.1), channel_id=2, replica_groups=mesh['elem'=8,'snap'=4] {'snap'}, dimensions={0}, use_global_device_ids=true | all-gather | bytes 491520 | tf_op jit(solution)/shard_map/all_gather | solution.py:388
  38.3 32.7 %panel.1 = (f32[16,128,512]{2,1,0:T(8,128)}, f32[64,512]{1,0:T(8,128)}) custom-call(s32[2]{0:T(128)} %pad_add_fusion.refs_0_.ids, bf16[4,96,512]{2,1,0:T(8,128)(2,1)} %bitcast.8, bf16[8,64,512]{2,1,0:T(8,128)(2,1)} %copy-done, f32[8,64]{1,0:T(8,128)} %get-tuple-element.5.owners, s32[1,64]{1,0:T(1,128)} %bitcast.13, bf16[16,24,24]{2,1,0:T(8,128)(2,1)} %stiff.1), custom_call_target="tpu_custom_call" | custom-call | tf_op jit(solution)/shard_map/panel/pallas_call | solution.py:390
Async XLA Ops:
  0.6 11.8 %copy-start.1 = (bf16[512,8]{0,1:T(8,128)(2,1)S(1)}, bf16[512,8]{0,1:T(8,128)(2,1)}, u32[]{:S(2)}) copy-start(bf16[512,8]{0,1:T(8,128)(2,1)} %param.9) | copy-start | bytes 24580
  5.2 21.8 %all-to-all-start = ((bf16[8,64,512]{2,1,0:T(8,128)(2,1)}), bf16[8,64,512]{2,1,0:T(8,128)(2,1)S(1)}, u32[]{:S(2)}, u32[]{:S(2)}) async-start(bf16[8,64,512]{2,1,0:T(8,128)(2,1)} %get-tuple-element.4), calls=%async_computation | async-start | bytes 1048576 | tf_op jit(solution)/shard_map/all_to_all | solution.py:377
  26.9 0.8 %copy-start = (bf16[8,64,512]{2,1,0:T(8,128)(2,1)}, bf16[8,64,512]{2,1,0:T(8,128)(2,1)S(1)}, u32[]{:S(2)}) copy-start(bf16[8,64,512]{2,1,0:T(8,128)(2,1)S(1)} %all-to-all-done.got) | copy-start | bytes 1572868

commit v2 on v1

v2 whole, which is shorter than its diff:
```python
import functools

import jax
import jax.numpy as jnp
from jax import lax
from jax.experimental import pallas as pl
from jax.experimental.pallas import tpu as pltpu
from jax.sharding import PartitionSpec as P

F32, BF16, I32 = jnp.float32, jnp.bfloat16, jnp.int32
NT = (((1,), (1,)), ((), ()))
NN = (((1,), (0,)), ((), ()))
TN = (((0,), (0,)), ((), ()))
LANES = 128
TILE = 256
BLOCK = 128
PANEL = 64
STEP = 8
MEBI = 1 << 20
JOINED_LIMIT = 1 << 22
ROWS_PER_TABLE = 512


def dot(a, b, dims=NN):
    return lax.dot_general(a, b, dims, preferred_element_type=F32)


def split(x):
    high = x.astype(BF16)
    return high, (x - high.astype(F32)).astype(BF16)


def dot3(a, b, dims=NN):
    (ah, al), (bh, bl) = a, b
    return dot(ah, bh, dims) + (dot(ah, bl, dims) + dot(al, bh, dims))


def iota(shape, dim):
    return lax.broadcasted_iota(I32, shape, dim)


def quotient(x, n):
    return jnp.floor((x.astype(F32) + 0.5) * (1.0 / n)).astype(I32)


def node_places(sample, links, table):
    positions, elems = links.shape
    sampled = sample.shape[1]
    pick = (iota((elems, sampled), 0) == sample).astype(F32).astype(BF16)
    shifted = links + 1
    parts = jnp.concatenate([(shifted >> 8).astype(F32), (shifted & 255).astype(F32)], axis=0)
    found = dot(parts.astype(BF16), pick)
    nodes = (found[:positions] * 256.0 + found[positions:]).astype(I32) - 1
    halves = jnp.concatenate([(table >> 8).astype(F32), (table & 255).astype(F32)], axis=1).T.astype(BF16)
    high, low = jnp.maximum(nodes, 0) >> 7, jnp.maximum(nodes, 0) & (LANES - 1)
    places = jnp.zeros((positions, sampled), F32)
    for p in range(positions):
        rows = (iota((table.shape[0], sampled), 0) == high[p : p + 1]).astype(F32).astype(BF16)
        both = dot(halves, rows)
        here = iota((LANES, sampled), 0) == low[p : p + 1]
        value = both[:LANES] * 256.0 + both[LANES:]
        value = jnp.sum(jnp.where(here, value, 0.0), axis=0, keepdims=True)
        places = jnp.where(iota((positions, sampled), 0) == p, value, places)
    return jnp.where(nodes >= 0, places, -1.0)


def slot_picks(elem_device, device, capacity):
    sampled = elem_device.shape[1]
    mine = (elem_device == device).astype(F32)
    before = (iota((sampled, sampled), 0) < iota((sampled, sampled), 1)).astype(F32).astype(BF16)
    ranks = dot(jnp.broadcast_to(mine, (16, sampled)).astype(BF16), before)[0:1]
    return jnp.where(iota((capacity, sampled), 0).astype(F32) == ranks, mine, 0.0)


def owner_kernel(devices, groups, capacity, ndof, *refs):
    inputs, outputs = refs[:5], refs[5:-6]
    *held, basis, sems = refs[-6:]
    shared, slots, owners = outputs[0], outputs[-2], outputs[-1]
    sample, links, table, elem_device = held[:4]
    modes = basis.shape[1] // ndof
    copies = [pltpu.make_async_copy(ref, to, sems.at[n]) for n, (ref, to) in enumerate(zip(inputs[:4], held))]
    for c in range(ndof):
        part = slice(c * modes, (c + 1) * modes)
        copies.append(pltpu.make_async_copy(inputs[4].at[:, part], basis.at[:, part], sems.at[4 + c]))
    for copy in copies:
        copy.start()
    elem_rank, snap_rank = lax.axis_index("elem"), lax.axis_index("snap")
    node_rows = basis.shape[0]
    band = modes // groups
    sampled = sample.shape[1]
    quarter = sampled // groups
    first = slots.shape[1] - capacity
    for copy in copies[:4]:
        copy.wait()
    places = node_places(sample[...], links[...], table[...])
    owner = jnp.floor((places + 0.5) * (1.0 / node_rows))
    owners[...] = jnp.where(places >= 0, owner, -1.0)
    here = (places >= 0) & (owner == elem_rank.astype(F32))
    local = places - (elem_rank * node_rows).astype(F32) + 1.0
    local = jnp.sum(jnp.where(here, local, 0.0), axis=0, keepdims=True)
    wanted = (iota((quarter, sampled), 1) == iota((quarter, sampled), 0) + snap_rank * quarter).astype(F32)
    picks = [wanted] + [slot_picks(elem_device[...], d, capacity) for d in range(devices)]
    row = jnp.sum(jnp.concatenate(picks, axis=0) * local, axis=1, keepdims=True).astype(I32) - 1
    pick = (iota((row.shape[0], node_rows), 1) == row).astype(F32).astype(BF16)
    for c in range(ndof):
        copies[4 + c].wait()
        rows = dot(pick, basis[:, c * modes : (c + 1) * modes])
        full = rows[:quarter].astype(BF16)
        part = jnp.zeros((devices * capacity, band), F32)
        for k in range(groups):
            part = jnp.where(snap_rank == k, rows[quarter:, k * band : (k + 1) * band], part)
        part = part.astype(BF16)
        for d in range(shared.shape[0]):
            shared[d, c * quarter : (c + 1) * quarter, :] = full
        for d in range(devices):
            slots[d, first:, c * band : (c + 1) * band] = part[d * capacity : (d + 1) * capacity]
    for d in range(devices):
        slots[d, first:, ndof * band :] = jnp.zeros((capacity, modes - ndof * band), BF16)


def place_targets(owner_col, ndof, pitch, live, members):
    index = iota(owner_col.shape, 0)
    member, row = index // pitch, index % pitch
    position = quotient(row, ndof)
    dof = row - position * ndof
    target = (owner_col.astype(I32) * ndof + dof) * members + member
    target = jnp.where((owner_col >= 0) & (row < live), target, -1)
    return jnp.broadcast_to(target, (owner_col.shape[0], LANES))


def one_hot(targets, lane_count, start=0):
    rows = targets.shape[0]
    wide = [iota((rows, LANES), 1) + (start + at) == targets for at in range(0, lane_count, LANES)]
    return jnp.concatenate([w.astype(F32).astype(BF16) for w in wide], axis=1)


def owner_rows(owners, rows, ndof, pitch):
    positions = owners.shape[0]
    position = quotient(iota((rows, positions), 0) % pitch, ndof)
    pick = (position == iota((rows, positions), 1)).astype(F32).astype(BF16)
    return dot(pick, owners.astype(BF16))


def table_kernel(ndof, pitch, groups, owners, elem_device, quarter_places, slot_places, slot_lane):
    elem_rank, snap_rank = lax.axis_index("elem"), lax.axis_index("snap")
    positions, sampled = owners.shape
    live = positions * ndof
    quarter = sampled // groups
    parts, rows, _ = quarter_places.shape
    members = rows // pitch
    own = owner_rows(owners[...], rows, ndof, pitch)
    for h in range(parts):
        first = snap_rank * quarter + h * members
        at = iota((rows, sampled), 1) == iota((rows, sampled), 0) // pitch + first
        owner_col = jnp.sum(jnp.where(at, own, 0.0), axis=1, keepdims=True)
        quarter_places[h] = place_targets(owner_col, ndof, pitch, live, members)

    rows = slot_places.shape[0]
    capacity = rows // pitch
    picks = slot_picks(elem_device[...], elem_rank, capacity)
    member = iota((rows, capacity), 0) // pitch
    expand = (member == iota((rows, capacity), 1)).astype(F32).astype(BF16)
    picks = dot(expand, picks.astype(BF16))
    own = owner_rows(owners[...], rows, ndof, pitch)
    owner_col = jnp.sum(picks * (own + 1.0), axis=1, keepdims=True) - 1.0
    slot_places[...] = place_targets(owner_col, ndof, pitch, live, capacity)
    which = jnp.sum(picks * (iota((rows, sampled), 1) + 1).astype(F32), axis=1, keepdims=True).astype(I32) - 1
    lane = which * pitch + iota((rows, 1), 0) % pitch
    slot_lane[...] = jnp.broadcast_to(jnp.where(which >= 0, lane, -1), (rows, LANES))


def element_kernel(ndof, pitch, got, coords, places, out):
    devices = got.shape[0]
    parts, rows, _ = places.shape
    members = rows // pitch
    quarter = parts * members
    snaps = out.shape[0] - 2 * pitch
    per_tile = TILE // pitch
    for h in range(parts):
        source = jnp.concatenate(
            [
                got[o, c * quarter + h * members : c * quarter + (h + 1) * members, :]
                for o in range(devices)
                for c in range(ndof)
            ],
            axis=0,
        )
        basis = dot(one_hot(places[h], source.shape[0]), source).astype(BF16)
        moved = dot(coords[...], basis, NT).astype(BF16)
        out[0:snaps, h * rows : (h + 1) * rows] = moved
        for g in range(rows // TILE):
            part = basis[g * TILE : (g + 1) * TILE]
            square = dot(part, part, NT)
            block = jnp.zeros((pitch, TILE), F32)
            for i in range(per_tile):
                inside = iota((pitch, TILE), 1) // pitch == i
                block = jnp.where(inside, square[i * pitch : (i + 1) * pitch], block)
            high, low = split(block)
            lanes = slice(h * rows + g * TILE, h * rows + (g + 1) * TILE)
            out[snaps : snaps + pitch, lanes] = high
            out[snaps + pitch :, lanes] = low


def spread(x):
    return jnp.broadcast_to(x, (STEP, LANES))


def factor_block(block, rows, work):
    count, per = BLOCK // STEP, PANEL // STEP
    span = range(STEP)
    left = [block[STEP * c : STEP * c + STEP] for c in range(count)]
    right = [
        (iota((STEP, LANES), 1) == iota((STEP, LANES), 0) + STEP * c).astype(F32) for c in range(count)
    ]
    sub = iota((STEP, LANES), 0)

    def columns_of(c, base):
        return [spread(left[c][:, base + k : base + k + 1]) for k in span]

    upper, inverse = [], []
    work = list(work)
    own = near = None
    for j in range(count):
        base = STEP * j
        end = (j // per + 1) * per
        rows[j, 0], rows[j, 1] = left[j], right[j]
        ul = [spread(rows[j, 0, k : k + 1]) for k in span]
        ur = [spread(rows[j, 1, k : k + 1]) for k in span]
        own = columns_of(j, base) if own is None else own
        for k in span:
            rows[j, 2 + k] = own[k]
        s = {(i, k): spread(rows[j, 2 + k, i : i + 1]) for k in span for i in range(k, STEP)}
        below = {c: columns_of(c, base) for c in range(j + 1, end)}
        if near is not None:
            below[j + 1] = near
        next_own = columns_of(j + 1, base + STEP) if j + 1 < end else None
        next_near = columns_of(j + 2, base + STEP) if j + 2 < end else None
        low = {}
        out_l, out_r = jnp.zeros((STEP, LANES), F32), jnp.zeros((STEP, LANES), F32)
        for k in span:
            root = lax.rsqrt(s[k, k])
            for i in range(k + 1, STEP):
                low[i, k] = s[i, k] * root
            for m in range(k + 1, STEP):
                for i in range(m, STEP):
                    s[i, m] = s[i, m] - low[i, k] * low[m, k]
            ul[k], ur[k] = ul[k] * root, ur[k] * root
            for i in range(k + 1, STEP):
                ul[i] = ul[i] - low[i, k] * ul[k]
                ur[i] = ur[i] - low[i, k] * ur[k]
            out_l = jnp.where(sub == k, ul[k], out_l)
            out_r = jnp.where(sub == k, ur[k], out_r)
            scaled = {}
            for c, col in below.items():
                scaled[c] = col[k] * root
                for i in range(k + 1, STEP):
                    col[i] = col[i] - scaled[c] * low[i, k]
                left[c] = left[c] - scaled[c] * ul[k]
                right[c] = right[c] - scaled[c] * ur[k]
            if next_own is not None:
                rows[j, 2 + STEP + k] = scaled[j + 1]
                for i in span:
                    other = spread(rows[j, 2 + STEP + k, i : i + 1])
                    next_own[i] = next_own[i] - scaled[j + 1] * other
                    if next_near is not None:
                        next_near[i] = next_near[i] - scaled[j + 2] * other
        own, near = next_own, next_near
        keep = iota((STEP, LANES), 1) >= sub + base
        upper.append(jnp.where(keep, out_l, 0.0))
        inverse.append(out_r)
        if j + 1 == end and end < count:
            lh, ll = split(jnp.concatenate(upper[end - per : end], axis=0))
            rh, rl = split(jnp.concatenate(inverse[end - per : end], axis=0))
            both_h, both_l = jnp.concatenate([lh, rh], axis=1), jnp.concatenate([ll, rl], axis=1)
            update = dot(
                jnp.concatenate([lh, lh, ll], axis=0), jnp.concatenate([both_h, both_l, both_h], axis=0), TN
            )
            for c in range(end, count):
                left[c] = left[c] - update[STEP * c : STEP * c + STEP, :LANES]
                right[c] = right[c] - update[STEP * c : STEP * c + STEP, LANES:]
        for _ in range(-(-len(work) // (count - j))):
            work.pop(0)()
    return jnp.concatenate(upper, axis=0), jnp.concatenate(inverse, axis=0)


def cut(b):
    return slice(b * BLOCK, (b + 1) * BLOCK)


def factorize(gram, side, lower, rows):
    count = gram.shape[0] // BLOCK
    block, work = gram[cut(0), cut(0)], []
    for b in range(count):
        top, inverse = factor_block(block, rows.at[b % 2], work)
        lower[cut(b), cut(b)] = top.T
        inverse, down, across, work = split(inverse), {}, {}, []

        def below(r, b=b, inverse=inverse, down=down):
            value = dot3(split(gram[cut(r), cut(b)]), inverse, NT)
            lower[cut(r), cut(b)] = value
            down[r] = split(value)

        def update(r, c, down=down):
            gram[cut(r), cut(c)] = gram[cut(r), cut(c)] - dot3(down[r], down[c], NT)

        def solve(h, b=b, inverse=inverse, across=across):
            value = dot3(inverse, split(side[cut(b), h : h + TILE]))
            side[cut(b), h : h + TILE] = value
            across[h] = split(value)

        def reduce(r, h, down=down, across=across):
            side[cut(r), h : h + TILE] = side[cut(r), h : h + TILE] - dot3(down[r], across[h])

        if b + 1 < count:
            below(b + 1)
            block = gram[cut(b + 1), cut(b + 1)] - dot3(down[b + 1], down[b + 1], NT)
        work = [functools.partial(below, r) for r in range(b + 2, count)]
        work += [functools.partial(update, r, c) for r in range(b + 2, count) for c in range(b + 1, r + 1)]
        for h in range(0, side.shape[1], TILE):
            work.append(functools.partial(solve, h))
            work += [functools.partial(reduce, r, h) for r in range(b + 1, count)]
    for step in work:
        step()


def panel_kernel(
    ndof, pitch, total_rows, every, got, places, slot_lane, stiff, panel, factor, forces, halves, gram, side,
    lower, turned, rows, result, sems,
):
    elem_rank = lax.axis_index("elem")
    groups, height, lanes = every.shape
    snaps = height - 2 * pitch
    terms, live, _ = stiff.shape
    columns = snaps * terms
    capacity, band, _ = panel.shape
    devices = got.shape[0]
    per_tile = TILE // pitch
    tiles = [(q, t) for q in range(groups) for t in range(lanes // TILE)]
    slot_rows = capacity * pitch
    slot_tiles = slot_rows // TILE
    chunk = 8

    first = got.shape[1] - capacity
    source = jnp.concatenate(
        [got[o, first:, c * band : (c + 1) * band] for o in range(devices) for c in range(ndof)], axis=0
    )
    basis_t = dot(one_hot(places[...], source.shape[0]), source).T

    slot_moved = jnp.zeros((snaps, slot_rows), F32)
    for n, (q, t) in enumerate(tiles):
        pick = one_hot(slot_lane[...], TILE, n * TILE)
        slot_moved = slot_moved + dot(every[q, 0:snaps, t * TILE : (t + 1) * TILE], pick, NT)
    slot_moved = slot_moved.astype(BF16)

    tile_of = (iota((live, TILE), 1) % pitch == iota((live, TILE), 0)).astype(F32).astype(BF16)
    diagonal = iota((TILE, TILE), 0) // pitch == iota((TILE, TILE), 1) // pitch
    terms_wide = []
    for t in range(terms):
        wide = dot(stiff[t], tile_of)
        wide = jnp.concatenate([wide, jnp.zeros((pitch - live, TILE), F32)], axis=0)
        wide = jnp.concatenate([wide] * per_tile, axis=0)
        terms_wide.append(jnp.where(diagonal, wide, 0.0).astype(BF16))

    def add_chunk(tiles, slot_part):
        def piece_of(q, t, first, count):
            return every[q, first : first + count, pl.ds(pl.multiple_of(t * TILE, TILE), TILE)]

        moved = [piece_of(q, t, 0, snaps) for q, t in tiles] + slot_part
        moved = jnp.concatenate(moved, axis=0)
        for t in range(terms):
            force = dot(moved, terms_wide[t], NT)
            for n in range(moved.shape[0] // snaps):
                for h in range(TILE // LANES):
                    piece = force[n * snaps : (n + 1) * snaps, h * LANES : (h + 1) * LANES]
                    forces[n * TILE // LANES + h, pl.ds(t, snaps, stride=terms), :] = piece
        end = len(tiles) * TILE
        for h in range(len(slot_part) * TILE // LANES):
            side[:, h * LANES : (h + 1) * LANES] = forces[end // LANES + h].astype(BF16).astype(F32)
        for n, (q, t) in enumerate(tiles):
            force = [forces[n * TILE // LANES + h] for h in range(TILE // LANES)]
            force = jnp.concatenate(force, axis=1).astype(BF16)
            total = None
            for low in (0, 1):
                square = piece_of(q, t, snaps + low * pitch, pitch)
                wide = jnp.concatenate([square.astype(F32)] * per_tile, axis=0)
                term = dot(force, jnp.where(diagonal, wide, 0.0).astype(BF16))
                total = term if total is None else total + term
            halves[0, :, n * TILE : (n + 1) * TILE] = force
            halves[1, :, n * TILE : (n + 1) * TILE], halves[2, :, n * TILE : (n + 1) * TILE] = split(total)
        for b in range(columns // BLOCK):
            upto = (b + 1) * BLOCK
            term = dot(halves[0, cut(b), :end], halves[1, :upto, :end], NT)
            term = term + dot(halves[0, cut(b), :end], halves[2, :upto, :end], NT)
            term = term * (1.0 / total_rows)
            gram[cut(b), :upto] = term if slot_part else gram[cut(b), :upto] + term

    add_chunk(tiles[:chunk], [slot_moved[:, t * TILE : (t + 1) * TILE] for t in range(slot_tiles)])
    per_group = lanes // TILE
    if len(tiles) > chunk:

        @pl.loop(1, len(tiles) // chunk)
        def _(step):
            numbers = [step * chunk + n for n in range(chunk)]
            add_chunk([(n // per_group, n % per_group) for n in numbers], [])

    for b in range(columns // BLOCK):
        for c in range(b):
            lower[cut(c), cut(b)] = jnp.zeros((BLOCK, BLOCK), F32)
    factorize(gram, side, lower, rows)

    share = factor.shape[0]
    block = elem_rank * share // BLOCK
    columns_here = lower[:, pl.ds(pl.multiple_of(block * BLOCK, BLOCK), BLOCK)]
    turned[...] = columns_here.T
    factor[...] = turned[pl.ds(pl.multiple_of(elem_rank * share - block * BLOCK, share), share), :]

    each = LANES // pitch
    copies = []
    for n in range(slot_rows // LANES):
        high, low = split(side[:, n * LANES : (n + 1) * LANES])
        right = jnp.concatenate([high, low], axis=1)
        piece = basis_t[:, n * LANES : (n + 1) * LANES]
        left = jnp.concatenate(
            [jnp.where(iota((band, LANES), 1) // pitch == i, piece, 0.0) for i in range(each)], axis=0
        ).astype(BF16)
        values = dot(jnp.concatenate([left, left], axis=1), right, NT)
        for i in range(each):
            result[n * each + i] = values[i * band : (i + 1) * band]
        here = pl.ds(n * each, each)
        copies.append(pltpu.make_async_copy(result.at[here], panel.at[here], sems.at[n]))
        copies[-1].start()
    for copy in copies:
        copy.wait()


def room(mebi, *arrays):
    size = sum(2 * a.size * a.dtype.itemsize for a in arrays)
    return pltpu.CompilerParams(vmem_limit_bytes=min(60 * MEBI, mebi * MEBI + size))


def shards(node_basis, stiff_terms, reduced_coords, sample_list, connectivity, node_slot, elem_device):
    devices = lax.axis_size("elem")
    groups = lax.axis_size("snap")
    node_rows, width = node_basis.shape
    modes, local_snaps = reduced_coords.shape
    snaps = local_snaps * groups
    ndof = width // modes
    terms, live, _ = stiff_terms.shape
    sampled = sample_list.shape[0]
    positions = connectivity.shape[1]
    capacity = 2 * sampled // devices
    quarter = sampled // groups
    pitch = 32
    band = modes // groups
    columns = snaps * terms
    total_rows = sampled * modes
    chunk_lanes = min(sampled * pitch, 8 * TILE)
    slot_rows = capacity * pitch

    vmem = pl.BlockSpec(memory_space=pltpu.VMEM)

    coords = lax.all_gather(reduced_coords.T, "snap", axis=0, tiled=True)
    sample_row = sample_list.reshape(1, sampled)
    device_row = elem_device.reshape(1, sampled)
    table = node_slot.reshape(-1, LANES)
    shared_rows = ndof * quarter
    joined = devices * (shared_rows + capacity) * modes <= JOINED_LIMIT
    if joined:
        sent = ((devices, shared_rows + capacity, modes),)
    else:
        sent = ((1, shared_rows, modes), (devices, capacity, modes))
    wanted = [jax.ShapeDtypeStruct(shape, BF16) for shape in sent]
    wanted.append(jax.ShapeDtypeStruct((positions, sampled), F32))
    taken = (sample_row, connectivity.T, table, device_row, node_basis)
    *sent, owners = pl.pallas_call(
        functools.partial(owner_kernel, devices, groups, capacity, ndof),
        out_shape=tuple(wanted),
        in_specs=[pl.BlockSpec(memory_space=pltpu.HBM)] * 5,
        out_specs=(vmem,) * len(wanted),
        scratch_shapes=[pltpu.VMEM(x.shape, x.dtype) for x in taken] + [pltpu.SemaphoreType.DMA((4 + ndof,))],
        compiler_params=room(60),
        name="owner_rows",
    )(*taken)
    slots = lax.all_to_all(sent[-1], "elem", split_axis=0, concat_axis=0, tiled=True)
    got = slots if joined else lax.all_gather(sent[0], "elem", axis=0, tiled=True)

    rows_per = ROWS_PER_TABLE
    members = rows_per // pitch
    tables = (
        jax.ShapeDtypeStruct((quarter // members, rows_per, LANES), I32),
        jax.ShapeDtypeStruct((slot_rows, LANES), I32),
        jax.ShapeDtypeStruct((slot_rows, LANES), I32),
    )
    quarter_places, slot_places, slot_lane = pl.pallas_call(
        functools.partial(table_kernel, ndof, pitch, groups),
        out_shape=tables,
        in_specs=[vmem] * 2,
        out_specs=(vmem,) * 3,
        compiler_params=room(8, *tables),
        name="place_tables",
    )(owners, device_row)
    mine = pl.pallas_call(
        functools.partial(element_kernel, ndof, pitch),
        out_shape=jax.ShapeDtypeStruct((snaps + 2 * pitch, quarter * pitch), BF16),
        in_specs=[vmem] * 3,
        out_specs=vmem,
        compiler_params=room(12, got, quarter_places),
        name="element_squares",
    )(got, coords, quarter_places)
    every = lax.all_gather(mine, "snap", axis=0)

    return pl.pallas_call(
        functools.partial(panel_kernel, ndof, pitch, total_rows),
        out_shape=(
            jax.ShapeDtypeStruct((capacity, band, columns), F32),
            jax.ShapeDtypeStruct((columns // devices, columns), F32),
        ),
        in_specs=[vmem] * 5,
        out_specs=(pl.BlockSpec(memory_space=pl.ANY), vmem),
        scratch_shapes=[
            pltpu.VMEM(((chunk_lanes + slot_rows) // LANES, columns, LANES), F32),
            pltpu.VMEM((3, columns, chunk_lanes), BF16),
            pltpu.VMEM((columns, columns), F32),
            pltpu.VMEM((columns, slot_rows), F32),
            pltpu.VMEM((columns, columns), F32),
            pltpu.VMEM((BLOCK, columns), F32),
            pltpu.VMEM((2, BLOCK // STEP, 2 + 2 * STEP, STEP, LANES), F32),
            pltpu.VMEM((capacity, band, columns), F32),
            pltpu.SemaphoreType.DMA((slot_rows // LANES,)),
        ],
        compiler_params=room(30, every, slot_places),
        name="panel",
    )(every, slots, slot_places, slot_lane, stiff_terms)


def solution(mesh):
    placed = (P("elem", None), P(), P(None, "snap"), P(), P(), P(), P())
    return jax.shard_map(
        shards,
        mesh=mesh,
        in_specs=placed,
        out_specs=(P("elem", "snap", None), P("elem", None)),
        check_vma=False,
    )
```

time: 71.3 us -> 55.7 us (0.78)
  Pallas kernels: 39.4 us -> 26.7 us
  blocking collectives: 13.4 us -> 11.8 us
  waiting for transfers between devices: 8.84 us -> 8.07 us
    pallas_call x1, Pallas kernels: 32.7 us -> 22 us  [shards(): pl.pallas_call(functools.partial(panel_kernel, ndof, pitch, total_rows),...]
    pallas_call x1, Pallas kernels: 2.75 us -> 0.84 us  [shards(): pl.pallas_call(functools.partial(element_kernel, ndof, pitch), out_shape=...]
    all_gather x1, blocking collectives: 7.79 us -> 6.64 us  [shards(): every = lax.all_gather(mine, 'snap', axis=0)]
    all_to_all x1, waiting for transfers between devices: 8.84 us -> 8.07 us  [shards(): lax.all_to_all(sent[-1], 'elem', split_axis=0, concat_axis=0, tiled=True)]
    pallas_call x1 -> x2, Pallas kernels: 3.94 us -> 3.79 us  [the longest x1 3.28 us: shards(): pl.pallas_call(functools.partial(owner_kernel, devices, groups, capacity,...]
  transfers between devices with their start and end apart: 1 -> 1, of which waited for: 1 -> 1; matrix products, arithmetic and copies ran while one was open for 0% -> 0% of each run, Pallas kernels for 0% -> 1%
where the time goes in v2:
time: 55.7 us; the launch traced here: 55.5 us
  Pallas kernels  26.7 us (48%)
  blocking collectives  11.8 us (21%)
  waiting for transfers between devices  8.07 us (14%)
  starting transfers between devices  7.3 us (13%)
  between operations  0.88 us (2%)
  local copies, waits for them, and re-layouts  0.69 us (1%)
    pallas_call x1, Pallas kernels, shards(): pl.pallas_call(functools.partial(panel_kernel, ndof, pitch, total_rows),...  22 us
    all_to_all x1, waiting for transfers between devices, shards(): lax.all_to_all(sent[-1], 'elem', split_axis=0, concat_axis=0, tiled=True)  8.07 us
    all_to_all x1, starting transfers between devices, shards(): lax.all_to_all(sent[-1], 'elem', split_axis=0, concat_axis=0, tiled=True)  7.3 us
    all_gather x1, blocking collectives, shards(): every = lax.all_gather(mine, 'snap', axis=0)  6.64 us
    all_gather x1, blocking collectives, shards(): coords = lax.all_gather(reduced_coords.T, 'snap', axis=0, tiled=True)  5.19 us
    pallas_call x1, Pallas kernels, shards(): pl.pallas_call(functools.partial(owner_kernel, devices, groups, capacity,...  3.28 us
  transfers between devices with their start and end apart: 1, of which 1 were waited for; matrix products, arithmetic and copies ran while one was open for 0% of the time, Pallas kernels for 1%

profile of v2, /device:TPU:0, one launch (start us, length us, event | category | flops | bytes accessed | tf_op | source)
XLA Modules:
  0.0 55.5 jit_solution(6244089276607831840)
XLA Ops:
  0.6 0.0 copy-start.2
  0.6 0.0 copy-start.3
  0.7 0.0 copy-start
  0.7 3.3 %owner_rows.1 = (bf16[8,64,512]{2,1,0:T(8,128)(2,1)}, f32[8,64]{1,0:T(8,128)}) custom-call(s32[1,64]{1,0:T(1,128)} %bitcast.12, s32[8,256]{1,0:T(8,128)} %bitcast.10, s32[64,128]{1,0:T(8,128)} %bitcast.9, s32[1,64]{1,0:T(1,128)} %bitcast.7, bf16[1024,1536]{1,0:T(8,128)(2,1)} %refs_4_.1), custom_call_target="tpu_custom_call" | custom-call | tf_op jit(solution)/shard_map/owner_rows/pallas_call | solution.py:475
  4.0 7.3 %all-to-all-start = ((bf16[8,64,512]{2,1,0:T(8,128)(2,1)}), bf16[8,64,512]{2,1,0:T(8,128)(2,1)S(1)}, u32[]{:S(2)}, u32[]{:S(2)}) async-start(bf16[8,64,512]{2,1,0:T(8,128)(2,1)} %get-tuple-element.7), calls=%async_computation | async-start | bytes 1048576 | tf_op jit(solution)/shard_map/all_to_all | solution.py:484
  11.2 0.0 copy-done.2
  11.3 0.0 copy-start.1
  11.3 0.7 %copy-done.1 = f32[8,64]{1,0:T(8,128)S(1)} copy-done((f32[8,64]{1,0:T(8,128)S(1)}, f32[8,64]{1,0:T(8,128)}, u32[]{:S(2)}) %copy-start.1) | copy-done | bytes 2072
  11.9 0.5 place_tables.1
  12.5 0.0 copy-done.3
  12.5 5.2 %all_gather.9.coords = bf16[32,512]{1,0:T(8,128)(2,1)S(1)} all-gather(bf16[8,512]{1,0:T(8,128)(2,1)S(1)} %bitcast.11), channel_id=1, replica_groups=mesh['elem'=8,'snap'=4] {'snap'}, dimensions={0}, use_global_device_ids=true | all-gather | bytes 40960 | tf_op jit(solution)/shard_map/all_gather | solution.py:462
  17.7 8.1 %all-to-all-done.got = bf16[8,64,512]{2,1,0:T(8,128)(2,1)S(1)} async-done(((bf16[8,64,512]{2,1,0:T(8,128)(2,1)}), bf16[8,64,512]{2,1,0:T(8,128)(2,1)S(1)}, u32[]{:S(2)}, u32[]{:S(2)}) %all-to-all-start) | async-done | bytes 524320 | tf_op jit(solution)/shard_map/all_to_all | solution.py:484
  25.7 0.8 %element_squares.1 = bf16[96,512]{1,0:T(8,128)(2,1)S(1)} custom-call(bf16[8,64,512]{2,1,0:T(8,128)(2,1)S(1)} %all-to-all-done.got, bf16[32,512]{1,0:T(8,128)(2,1)S(1)} %all_gather.9.coords, s32[1,512,128]{2,1,0:T(8,128)S(1)} %get-tuple-element.9.places), custom_call_target="tpu_custom_call" | custom-call | tf_op jit(solution)/shard_map/element_squares/pallas_call | solution.py:502
  26.6 6.6 %all-gather = bf16[384,512]{1,0:T(8,128)(2,1)S(1)} all-gather(bf16[96,512]{1,0:T(8,128)(2,1)S(1)} %element_squares.1), channel_id=2, replica_groups=mesh['elem'=8,'snap'=4] {'snap'}, dimensions={0}, use_global_device_ids=true | all-gather | bytes 491520 | tf_op jit(solution)/shard_map/all_gather | solution.py:510
  33.2 0.0 copy-done
  33.2 22.0 %panel.1 = (f32[16,128,512]{2,1,0:T(8,128)}, f32[64,512]{1,0:T(8,128)}) custom-call(bf16[4,96,512]{2,1,0:T(8,128)(2,1)S(1)} %bitcast.6, bf16[8,64,512]{2,1,0:T(8,128)(2,1)S(1)} %all-to-all-done.got, s32[512,128]{1,0:T(8,128)S(1)} %get-tuple-element.10.places, s32[512,128]{1,0:T(8,128)S(1)} %get-tuple-element.11.slot_lane, bf16[16,24,24]{2,1,0:T(8,128)(2,1)S(1)} %copy-done), custom_call_target="tpu_custom_call" | custom-call | tf_op jit(solution)/shard_map/panel/pallas_call | solution.py:512
Async XLA Ops:
  0.6 10.6 %copy-start.2 = (s32[64]{0:T(128)S(1)}, s32[64]{0:T(128)}, u32[]{:S(2)}) copy-start(s32[64]{0:T(128)} %param.13) | copy-start | bytes 772
  0.6 11.8 %copy-start.3 = (bf16[512,8]{0,1:T(8,128)(2,1)S(1)}, bf16[512,8]{0,1:T(8,128)(2,1)}, u32[]{:S(2)}) copy-start(bf16[512,8]{0,1:T(8,128)(2,1)} %param.9) | copy-start | bytes 24580
  0.7 32.6 %copy-start = (bf16[16,24,24]{2,1,0:T(8,128)(2,1)S(1)}, bf16[16,24,24]{2,1,0:T(8,128)(2,1)}, u32[]{:S(2)}) copy-start(bf16[16,24,24]{2,1,0:T(8,128)(2,1)} %stiff.1) | copy-start | bytes 55300
  4.0 21.8 %all-to-all-start = ((bf16[8,64,512]{2,1,0:T(8,128)(2,1)}), bf16[8,64,512]{2,1,0:T(8,128)(2,1)S(1)}, u32[]{:S(2)}, u32[]{:S(2)}) async-start(bf16[8,64,512]{2,1,0:T(8,128)(2,1)} %get-tuple-element.7), calls=%async_computation | async-start | bytes 1048576 | tf_op jit(solution)/shard_map/all_to_all | solution.py:484
  11.3 0.7 %copy-start.1 = (f32[8,64]{1,0:T(8,128)S(1)}, f32[8,64]{1,0:T(8,128)}, u32[]{:S(2)}) copy-start(f32[8,64]{1,0:T(8,128)} %get-tuple-element.8.owners) | copy-start | bytes 6148

commit v3 on v2

--- a/solution.py
+++ b/solution.py
@@ -19,6 +19,7 @@
 MEBI = 1 << 20
 JOINED_LIMIT = 1 << 22
 ROWS_PER_TABLE = 512
+CHUNK = 8
 
 
 def dot(a, b, dims=NN):
@@ -141,7 +142,9 @@
     return dot(pick, owners.astype(BF16))
 
 
-def table_kernel(ndof, pitch, groups, owners, elem_device, quarter_places, slot_places, slot_lane):
+def table_kernel(
+    ndof, pitch, groups, owners, elem_device, stiff, quarter_places, slot_places, slot_lane, terms_wide
+):
     elem_rank, snap_rank = lax.axis_index("elem"), lax.axis_index("snap")
     positions, sampled = owners.shape
     live = positions * ndof
@@ -167,6 +170,14 @@
     which = jnp.sum(picks * (iota((rows, sampled), 1) + 1).astype(F32), axis=1, keepdims=True).astype(I32) - 1
     lane = which * pitch + iota((rows, 1), 0) % pitch
     slot_lane[...] = jnp.broadcast_to(jnp.where(which >= 0, lane, -1), (rows, LANES))
+
+    tile_of = (iota((live, TILE), 1) % pitch == iota((live, TILE), 0)).astype(F32).astype(BF16)
+    diagonal = iota((TILE, TILE), 0) // pitch == iota((TILE, TILE), 1) // pitch
+    for t in range(stiff.shape[0]):
+        wide = dot(stiff[t], tile_of)
+        wide = jnp.concatenate([wide, jnp.zeros((pitch - live, TILE), F32)], axis=0)
+        wide = jnp.concatenate([wide] * (TILE // pitch), axis=0)
+        terms_wide[t] = jnp.where(diagonal, wide, 0.0).astype(BF16)
 
 
 def element_kernel(ndof, pitch, got, coords, places, out):
@@ -219,7 +230,7 @@
 
     upper, inverse = [], []
     work = list(work)
-    own = near = None
+    own = None
     for j in range(count):
         base = STEP * j
         end = (j // per + 1) * per
@@ -231,10 +242,7 @@
             rows[j, 2 + k] = own[k]
         s = {(i, k): spread(rows[j, 2 + k, i : i + 1]) for k in span for i in range(k, STEP)}
         below = {c: columns_of(c, base) for c in range(j + 1, end)}
-        if near is not None:
-            below[j + 1] = near
         next_own = columns_of(j + 1, base + STEP) if j + 1 < end else None
-        next_near = columns_of(j + 2, base + STEP) if j + 2 < end else None
         low = {}
         out_l, out_r = jnp.zeros((STEP, LANES), F32), jnp.zeros((STEP, LANES), F32)
         for k in span:
@@ -262,9 +270,7 @@
                 for i in span:
                     other = spread(rows[j, 2 + STEP + k, i : i + 1])
                     next_own[i] = next_own[i] - scaled[j + 1] * other
-                    if next_near is not None:
-                        next_near[i] = next_near[i] - scaled[j + 2] * other
-        own, near = next_own, next_near
+        own = next_own
         keep = iota((STEP, LANES), 1) >= sub + base
         upper.append(jnp.where(keep, out_l, 0.0))
         inverse.append(out_r)
@@ -287,9 +293,9 @@
     return slice(b * BLOCK, (b + 1) * BLOCK)
 
 
-def factorize(gram, side, lower, rows):
+def factorize(gram, side, lower, rows, work):
     count = gram.shape[0] // BLOCK
-    block, work = gram[cut(0), cut(0)], []
+    block = gram[cut(0), cut(0)]
     for b in range(count):
         top, inverse = factor_block(block, rows.at[b % 2], work)
         lower[cut(b), cut(b)] = top.T
@@ -324,89 +330,107 @@
 
 
 def panel_kernel(
-    ndof, pitch, total_rows, every, got, places, slot_lane, stiff, panel, factor, forces, halves, gram, side,
-    lower, turned, rows, result, sems,
+    ndof, pitch, total_rows, every, got, places, slot_lane, terms_wide, panel, factor, forces, halves, squares, gram,
+    side, lower, turned, rows, result, sems,
 ):
     elem_rank = lax.axis_index("elem")
     groups, height, lanes = every.shape
     snaps = height - 2 * pitch
-    terms, live, _ = stiff.shape
+    terms = terms_wide.shape[0]
     columns = snaps * terms
+    blocks = columns // BLOCK
     capacity, band, _ = panel.shape
     devices = got.shape[0]
-    per_tile = TILE // pitch
-    tiles = [(q, t) for q in range(groups) for t in range(lanes // TILE)]
+    per_tile, per_group = TILE // pitch, lanes // TILE
+    tiles = [(q, t) for q in range(groups) for t in range(per_group)]
     slot_rows = capacity * pitch
-    slot_tiles = slot_rows // TILE
-    chunk = 8
-
-    first = got.shape[1] - capacity
-    source = jnp.concatenate(
-        [got[o, first:, c * band : (c + 1) * band] for o in range(devices) for c in range(ndof)], axis=0
-    )
-    basis_t = dot(one_hot(places[...], source.shape[0]), source).T
-
-    slot_moved = jnp.zeros((snaps, slot_rows), F32)
-    for n, (q, t) in enumerate(tiles):
-        pick = one_hot(slot_lane[...], TILE, n * TILE)
-        slot_moved = slot_moved + dot(every[q, 0:snaps, t * TILE : (t + 1) * TILE], pick, NT)
-    slot_moved = slot_moved.astype(BF16)
-
-    tile_of = (iota((live, TILE), 1) % pitch == iota((live, TILE), 0)).astype(F32).astype(BF16)
     diagonal = iota((TILE, TILE), 0) // pitch == iota((TILE, TILE), 1) // pitch
-    terms_wide = []
-    for t in range(terms):
-        wide = dot(stiff[t], tile_of)
-        wide = jnp.concatenate([wide, jnp.zeros((pitch - live, TILE), F32)], axis=0)
-        wide = jnp.concatenate([wide] * per_tile, axis=0)
-        terms_wide.append(jnp.where(diagonal, wide, 0.0).astype(BF16))
-
-    def add_chunk(tiles, slot_part):
-        def piece_of(q, t, first, count):
-            return every[q, first : first + count, pl.ds(pl.multiple_of(t * TILE, TILE), TILE)]
-
-        moved = [piece_of(q, t, 0, snaps) for q, t in tiles] + slot_part
-        moved = jnp.concatenate(moved, axis=0)
+    held = {}
+
+    def piece_of(q, t, first, count):
+        return every[q, first : first + count, pl.ds(pl.multiple_of(t * TILE, TILE), TILE)]
+
+    def put_forces(moved, first):
+        count = moved.shape[0] // snaps
         for t in range(terms):
             force = dot(moved, terms_wide[t], NT)
-            for n in range(moved.shape[0] // snaps):
+            for n in range(count):
                 for h in range(TILE // LANES):
                     piece = force[n * snaps : (n + 1) * snaps, h * LANES : (h + 1) * LANES]
-                    forces[n * TILE // LANES + h, pl.ds(t, snaps, stride=terms), :] = piece
-        end = len(tiles) * TILE
-        for h in range(len(slot_part) * TILE // LANES):
-            side[:, h * LANES : (h + 1) * LANES] = forces[end // LANES + h].astype(BF16).astype(F32)
+                    forces[(first + n) * TILE // LANES + h, pl.ds(t, snaps, stride=terms), :] = piece
+
+    def start_chunk(part):
+        put_forces(jnp.concatenate([piece_of(q, t, 0, snaps) for q, t in part], axis=0), 0)
+        for n, (q, t) in enumerate(part):
+            for low in (0, 1):
+                square = piece_of(q, t, snaps + low * pitch, pitch).astype(F32)
+                wide = jnp.concatenate([square] * per_tile, axis=0)
+                squares[low, n] = jnp.where(diagonal, wide, 0.0).astype(BF16)
+
+    def multiply(b, n):
+        force = [forces[n * TILE // LANES + h, cut(b)] for h in range(TILE // LANES)]
+        force = jnp.concatenate(force, axis=1).astype(BF16)
+        here = slice(n * TILE, (n + 1) * TILE)
+        halves[0, cut(b), here] = force
+        halves[1, cut(b), here], halves[2, cut(b), here] = split(
+            dot(force, squares[0, n]) + dot(force, squares[1, n])
+        )
+
+    def add_gram(b, count, fresh):
+        end, upto = count * TILE, (b + 1) * BLOCK
+        term = dot(halves[0, cut(b), :end], halves[1, :upto, :end], NT)
+        term = term + dot(halves[0, cut(b), :end], halves[2, :upto, :end], NT)
+        term = term * (1.0 / total_rows)
+        gram[cut(b), :upto] = term if fresh else gram[cut(b), :upto] + term
+
+    def chunk_work(b, count, fresh):
+        work = [functools.partial(multiply, b, n) for n in range(count)]
+        return work + [functools.partial(add_gram, b, count, fresh)]
+
+    def slot_displaced():
+        moved = jnp.zeros((snaps, slot_rows), F32)
         for n, (q, t) in enumerate(tiles):
-            force = [forces[n * TILE // LANES + h] for h in range(TILE // LANES)]
-            force = jnp.concatenate(force, axis=1).astype(BF16)
-            total = None
-            for low in (0, 1):
-                square = piece_of(q, t, snaps + low * pitch, pitch)
-                wide = jnp.concatenate([square.astype(F32)] * per_tile, axis=0)
-                term = dot(force, jnp.where(diagonal, wide, 0.0).astype(BF16))
-                total = term if total is None else total + term
-            halves[0, :, n * TILE : (n + 1) * TILE] = force
-            halves[1, :, n * TILE : (n + 1) * TILE], halves[2, :, n * TILE : (n + 1) * TILE] = split(total)
-        for b in range(columns // BLOCK):
-            upto = (b + 1) * BLOCK
-            term = dot(halves[0, cut(b), :end], halves[1, :upto, :end], NT)
-            term = term + dot(halves[0, cut(b), :end], halves[2, :upto, :end], NT)
-            term = term * (1.0 / total_rows)
-            gram[cut(b), :upto] = term if slot_part else gram[cut(b), :upto] + term
-
-    add_chunk(tiles[:chunk], [slot_moved[:, t * TILE : (t + 1) * TILE] for t in range(slot_tiles)])
-    per_group = lanes // TILE
-    if len(tiles) > chunk:
-
-        @pl.loop(1, len(tiles) // chunk)
+            moved = moved + dot(piece_of(q, t, 0, snaps), one_hot(slot_lane[...], TILE, n * TILE), NT)
+        moved = moved.astype(BF16)
+        moved = [moved[:, t * TILE : (t + 1) * TILE] for t in range(slot_rows // TILE)]
+        held["moved"] = jnp.concatenate(moved, axis=0)
+
+    def slot_forces():
+        put_forces(held["moved"], CHUNK)
+        for h in range(slot_rows // LANES):
+            side[:, h * LANES : (h + 1) * LANES] = forces[CHUNK * TILE // LANES + h].astype(BF16).astype(F32)
+
+    def slot_basis():
+        first = got.shape[1] - capacity
+        source = jnp.concatenate(
+            [got[o, first:, c * band : (c + 1) * band] for o in range(devices) for c in range(ndof)], axis=0
+        )
+        held["basis"] = dot(one_hot(places[...], source.shape[0]), source).T
+
+    def clear():
+        for b in range(blocks):
+            for c in range(b):
+                lower[cut(c), cut(b)] = jnp.zeros((BLOCK, BLOCK), F32)
+
+    slot_work = [slot_displaced, slot_forces, slot_basis, clear]
+    if len(tiles) <= CHUNK:
+        start_chunk(tiles)
+        for step in chunk_work(0, len(tiles), True):
+            step()
+        work = [step for b in range(1, blocks) for step in chunk_work(b, len(tiles), True)] + slot_work
+    else:
+        gram[...] = jnp.zeros_like(gram)
+
+        @pl.loop(0, len(tiles) // CHUNK)
         def _(step):
-            numbers = [step * chunk + n for n in range(chunk)]
-            add_chunk([(n // per_group, n % per_group) for n in numbers], [])
-
-    for b in range(columns // BLOCK):
-        for c in range(b):
-            lower[cut(c), cut(b)] = jnp.zeros((BLOCK, BLOCK), F32)
-    factorize(gram, side, lower, rows)
+            numbers = [step * CHUNK + n for n in range(CHUNK)]
+            start_chunk([(n // per_group, n % per_group) for n in numbers])
+            for b in range(blocks):
+                for work in chunk_work(b, CHUNK, False):
+                    work()
+
+        work = slot_work
+    factorize(gram, side, lower, rows, work)
 
     share = factor.shape[0]
     block = elem_rank * share // BLOCK
@@ -419,7 +443,7 @@
     for n in range(slot_rows // LANES):
         high, low = split(side[:, n * LANES : (n + 1) * LANES])
         right = jnp.concatenate([high, low], axis=1)
-        piece = basis_t[:, n * LANES : (n + 1) * LANES]
+        piece = held["basis"][:, n * LANES : (n + 1) * LANES]
         left = jnp.concatenate(
             [jnp.where(iota((band, LANES), 1) // pitch == i, piece, 0.0) for i in range(each)], axis=0
         ).astype(BF16)
@@ -454,7 +478,7 @@
     band = modes // groups
     columns = snaps * terms
     total_rows = sampled * modes
-    chunk_lanes = min(sampled * pitch, 8 * TILE)
+    chunk_lanes = CHUNK * TILE
     slot_rows = capacity * pitch
 
     vmem = pl.BlockSpec(memory_space=pltpu.VMEM)
@@ -490,15 +514,16 @@
         jax.ShapeDtypeStruct((quarter // members, rows_per, LANES), I32),
         jax.ShapeDtypeStruct((slot_rows, LANES), I32),
         jax.ShapeDtypeStruct((slot_rows, LANES), I32),
+        jax.ShapeDtypeStruct((terms, TILE, TILE), BF16),
     )
-    quarter_places, slot_places, slot_lane = pl.pallas_call(
+    quarter_places, slot_places, slot_lane, terms_wide = pl.pallas_call(
         functools.partial(table_kernel, ndof, pitch, groups),
         out_shape=tables,
-        in_specs=[vmem] * 2,
-        out_specs=(vmem,) * 3,
-        compiler_params=room(8, *tables),
+        in_specs=[vmem] * 3,
+        out_specs=(vmem,) * 4,
+        compiler_params=room(14, *tables),
         name="place_tables",
-    )(owners, device_row)
+    )(owners, device_row, stiff_terms)
     mine = pl.pallas_call(
         functools.partial(element_kernel, ndof, pitch),
         out_shape=jax.ShapeDtypeStruct((snaps + 2 * pitch, quarter * pitch), BF16),
@@ -520,6 +545,7 @@
         scratch_shapes=[
             pltpu.VMEM(((chunk_lanes + slot_rows) // LANES, columns, LANES), F32),
             pltpu.VMEM((3, columns, chunk_lanes), BF16),
+            pltpu.VMEM((2, CHUNK, TILE, TILE), BF16),
             pltpu.VMEM((columns, columns), F32),
             pltpu.VMEM((columns, slot_rows), F32),
             pltpu.VMEM((columns, columns), F32),
@@ -528,9 +554,9 @@
             pltpu.VMEM((capacity, band, columns), F32),
             pltpu.SemaphoreType.DMA((slot_rows // LANES,)),
         ],
-        compiler_params=room(30, every, slot_places),
+        compiler_params=room(34, every, slot_places),
         name="panel",
-    )(every, slots, slot_places, slot_lane, stiff_terms)
+    )(every, slots, slot_places, slot_lane, terms_wide)
 
 
 def solution(mesh):

time: 55.7 us -> 54.5 us (0.978)
  Pallas kernels: 26.7 us -> 25.6 us
    pallas_call x1, Pallas kernels: 22 us -> 20.8 us  [shards(): pl.pallas_call(functools.partial(panel_kernel, ndof, pitch, total_rows),...]
where the time goes in v3:
time: 54.5 us; the launch traced here: 54.2 us
  Pallas kernels  25.6 us (47%)
  blocking collectives  11.8 us (22%)
  waiting for transfers between devices  7.88 us (14%)
  starting transfers between devices  7.3 us (13%)
  between operations  0.89 us (2%)
  local copies, waits for them, and re-layouts  0.69 us (1%)
    pallas_call x1, Pallas kernels, shards(): pl.pallas_call(functools.partial(panel_kernel, ndof, pitch, total_rows),...  20.8 us
    all_to_all x1, waiting for transfers between devices, shards(): lax.all_to_all(sent[-1], 'elem', split_axis=0, concat_axis=0, tiled=True)  7.88 us
    all_to_all x1, starting transfers between devices, shards(): lax.all_to_all(sent[-1], 'elem', split_axis=0, concat_axis=0, tiled=True)  7.3 us
    all_gather x1, blocking collectives, shards(): every = lax.all_gather(mine, 'snap', axis=0)  6.65 us
    all_gather x1, blocking collectives, shards(): coords = lax.all_gather(reduced_coords.T, 'snap', axis=0, tiled=True)  5.19 us
    pallas_call x1, Pallas kernels, shards(): pl.pallas_call(functools.partial(owner_kernel, devices, groups, capacity,...  3.29 us
  transfers between devices with their start and end apart: 1, of which 1 were waited for; matrix products, arithmetic and copies ran while one was open for 0% of the time, Pallas kernels for 1%

profile of v3, /device:TPU:0, one launch (start us, length us, event | category | flops | bytes accessed | tf_op | source)
XLA Modules:
  0.0 54.2 jit_solution(4712249455643053746)
XLA Ops:
  0.6 0.0 copy-start.2
  0.6 0.0 copy-start
  0.7 0.0 copy-start.3
  0.7 3.3 %owner_rows.1 = (bf16[8,64,512]{2,1,0:T(8,128)(2,1)}, f32[8,64]{1,0:T(8,128)}) custom-call(s32[1,64]{1,0:T(1,128)} %bitcast.12, s32[8,256]{1,0:T(8,128)} %bitcast.10, s32[64,128]{1,0:T(8,128)} %bitcast.9, s32[1,64]{1,0:T(1,128)} %bitcast.7, bf16[1024,1536]{1,0:T(8,128)(2,1)} %refs_4_.1), custom_call_target="tpu_custom_call" | custom-call | tf_op jit(solution)/shard_map/owner_rows/pallas_call | solution.py:499
  4.0 7.3 %all-to-all-start = ((bf16[8,64,512]{2,1,0:T(8,128)(2,1)}), bf16[8,64,512]{2,1,0:T(8,128)(2,1)S(1)}, u32[]{:S(2)}, u32[]{:S(2)}) async-start(bf16[8,64,512]{2,1,0:T(8,128)(2,1)} %get-tuple-element.8), calls=%async_computation | async-start | bytes 1048576 | tf_op jit(solution)/shard_map/all_to_all | solution.py:508
  11.3 0.0 copy-done.2
  11.3 0.0 copy-done
  11.3 0.0 copy-start.1
  11.3 0.7 %copy-done.1 = f32[8,64]{1,0:T(8,128)S(1)} copy-done((f32[8,64]{1,0:T(8,128)S(1)}, f32[8,64]{1,0:T(8,128)}, u32[]{:S(2)}) %copy-start.1) | copy-done | bytes 2072
  12.0 0.7 %place_tables.1 = (s32[1,512,128]{2,1,0:T(8,128)S(1)}, s32[512,128]{1,0:T(8,128)S(1)}, s32[512,128]{1,0:T(8,128)S(1)}, bf16[16,256,256]{2,1,0:T(8,128)(2,1)S(1)}) custom-call(f32[8,64]{1,0:T(8,128)S(1)} %copy-done.1, s32[1,64]{1,0:T(1,128)S(1)} %bitcast.8, bf16[16,24,24]{2,1,0:T(8,128)(2,1)S(1)} %copy-done), custom_call_target="tpu_custom_call" | custom-call | tf_op jit(solution)/shard_map/place_tables/pallas_call | solution.py:519
  12.7 0.0 copy-done.3
  12.7 5.2 %all_gather.9.coords = bf16[32,512]{1,0:T(8,128)(2,1)S(1)} all-gather(bf16[8,512]{1,0:T(8,128)(2,1)S(1)} %bitcast.11), channel_id=1, replica_groups=mesh['elem'=8,'snap'=4] {'snap'}, dimensions={0}, use_global_device_ids=true | all-gather | bytes 40960 | tf_op jit(solution)/shard_map/all_gather | solution.py:486
  17.9 7.9 %all-to-all-done.got = bf16[8,64,512]{2,1,0:T(8,128)(2,1)S(1)} async-done(((bf16[8,64,512]{2,1,0:T(8,128)(2,1)}), bf16[8,64,512]{2,1,0:T(8,128)(2,1)S(1)}, u32[]{:S(2)}, u32[]{:S(2)}) %all-to-all-start) | async-done | bytes 524320 | tf_op jit(solution)/shard_map/all_to_all | solution.py:508
  25.7 0.8 %element_squares.1 = bf16[96,512]{1,0:T(8,128)(2,1)S(1)} custom-call(bf16[8,64,512]{2,1,0:T(8,128)(2,1)S(1)} %all-to-all-done.got, bf16[32,512]{1,0:T(8,128)(2,1)S(1)} %all_gather.9.coords, s32[1,512,128]{2,1,0:T(8,128)S(1)} %get-tuple-element.10.places), custom_call_target="tpu_custom_call" | custom-call | tf_op jit(solution)/shard_map/element_squares/pallas_call | solution.py:527
  26.6 6.6 %all-gather = bf16[384,512]{1,0:T(8,128)(2,1)S(1)} all-gather(bf16[96,512]{1,0:T(8,128)(2,1)S(1)} %element_squares.1), channel_id=2, replica_groups=mesh['elem'=8,'snap'=4] {'snap'}, dimensions={0}, use_global_device_ids=true | all-gather | bytes 491520 | tf_op jit(solution)/shard_map/all_gather | solution.py:535
  33.2 20.8 %panel.1 = (f32[16,128,512]{2,1,0:T(8,128)}, f32[64,512]{1,0:T(8,128)}) custom-call(bf16[4,96,512]{2,1,0:T(8,128)(2,1)S(1)} %bitcast.6, bf16[8,64,512]{2,1,0:T(8,128)(2,1)S(1)} %all-to-all-done.got, s32[512,128]{1,0:T(8,128)S(1)} %get-tuple-element.11.places, s32[512,128]{1,0:T(8,128)S(1)} %get-tuple-element.12.slot_lane, ...), custom_call_target="tpu_custom_call" | custom-call | tf_op jit(solution)/shard_map/panel/pallas_call | solution.py:537
Async XLA Ops:
  0.6 10.6 %copy-start.2 = (s32[64]{0:T(128)S(1)}, s32[64]{0:T(128)}, u32[]{:S(2)}) copy-start(s32[64]{0:T(128)} %param.13) | copy-start | bytes 772
  0.6 10.6 %copy-start = (bf16[16,24,24]{2,1,0:T(8,128)(2,1)S(1)}, bf16[16,24,24]{2,1,0:T(8,128)(2,1)}, u32[]{:S(2)}) copy-start(bf16[16,24,24]{2,1,0:T(8,128)(2,1)} %stiff.1) | copy-start | bytes 55300
  0.7 12.0 %copy-start.3 = (bf16[512,8]{0,1:T(8,128)(2,1)S(1)}, bf16[512,8]{0,1:T(8,128)(2,1)}, u32[]{:S(2)}) copy-start(bf16[512,8]{0,1:T(8,128)(2,1)} %param.9) | copy-start | bytes 24580
  4.0 21.8 %all-to-all-start = ((bf16[8,64,512]{2,1,0:T(8,128)(2,1)}), bf16[8,64,512]{2,1,0:T(8,128)(2,1)S(1)}, u32[]{:S(2)}, u32[]{:S(2)}) async-start(bf16[8,64,512]{2,1,0:T(8,128)(2,1)} %get-tuple-element.8), calls=%async_computation | async-start | bytes 1048576 | tf_op jit(solution)/shard_map/all_to_all | solution.py:508
  11.3 0.7 %copy-start.1 = (f32[8,64]{1,0:T(8,128)S(1)}, f32[8,64]{1,0:T(8,128)}, u32[]{:S(2)}) copy-start(f32[8,64]{1,0:T(8,128)} %get-tuple-element.9.owners) | copy-start | bytes 6148

commit v4 on v3

--- a/solution.py
+++ b/solution.py
@@ -33,7 +33,9 @@
 
 def dot3(a, b, dims=NN):
     (ah, al), (bh, bl) = a, b
-    return dot(ah, bh, dims) + (dot(ah, bl, dims) + dot(al, bh, dims))
+    (along,), (across,) = dims[0]
+    left = jnp.concatenate([ah, ah, al], axis=along)
+    return dot(left, jnp.concatenate([bh, bl, bh], axis=across), dims)
 
 
 def iota(shape, dim):
@@ -372,15 +374,14 @@
         force = jnp.concatenate(force, axis=1).astype(BF16)
         here = slice(n * TILE, (n + 1) * TILE)
         halves[0, cut(b), here] = force
-        halves[1, cut(b), here], halves[2, cut(b), here] = split(
-            dot(force, squares[0, n]) + dot(force, squares[1, n])
-        )
+        both = jnp.concatenate([squares[0, n], squares[1, n]], axis=0)
+        halves[1, cut(b), here], halves[2, cut(b), here] = split(dot(jnp.concatenate([force, force], axis=1), both))
 
     def add_gram(b, count, fresh):
         end, upto = count * TILE, (b + 1) * BLOCK
-        term = dot(halves[0, cut(b), :end], halves[1, :upto, :end], NT)
-        term = term + dot(halves[0, cut(b), :end], halves[2, :upto, :end], NT)
-        term = term * (1.0 / total_rows)
+        force = halves[0, cut(b), :end]
+        both = jnp.concatenate([halves[1, :upto, :end], halves[2, :upto, :end]], axis=1)
+        term = dot(jnp.concatenate([force, force], axis=1), both, NT) * (1.0 / total_rows)
         gram[cut(b), :upto] = term if fresh else gram[cut(b), :upto] + term
 
     def chunk_work(b, count, fresh):
@@ -398,7 +399,8 @@
     def slot_forces():
         put_forces(held["moved"], CHUNK)
         for h in range(slot_rows // LANES):
-            side[:, h * LANES : (h + 1) * LANES] = forces[CHUNK * TILE // LANES + h].astype(BF16).astype(F32)
+            force = forces[CHUNK * TILE // LANES + h, :columns]
+            side[:, h * LANES : (h + 1) * LANES] = force.astype(BF16).astype(F32)
 
     def slot_basis():
         first = got.shape[1] - capacity
@@ -543,7 +545,7 @@
         in_specs=[vmem] * 5,
         out_specs=(pl.BlockSpec(memory_space=pl.ANY), vmem),
         scratch_shapes=[
-            pltpu.VMEM(((chunk_lanes + slot_rows) // LANES, columns, LANES), F32),
+            pltpu.VMEM(((chunk_lanes + slot_rows) // LANES, columns + terms, LANES), F32),
             pltpu.VMEM((3, columns, chunk_lanes), BF16),
             pltpu.VMEM((2, CHUNK, TILE, TILE), BF16),
             pltpu.VMEM((columns, columns), F32),

time: 54.5 us -> 54.1 us (level)
  no operation moved by 1% of the time
where the time goes in v4:
time: 54.1 us; the launch traced here: 53.8 us
  Pallas kernels  25.2 us (47%)
  blocking collectives  11.8 us (22%)
  waiting for transfers between devices  7.88 us (15%)
  starting transfers between devices  7.3 us (13%)
  between operations  0.89 us (2%)
  local copies, waits for them, and re-layouts  0.69 us (1%)
    pallas_call x1, Pallas kernels, shards(): pl.pallas_call(functools.partial(panel_kernel, ndof, pitch, total_rows),...  20.4 us
    all_to_all x1, waiting for transfers between devices, shards(): lax.all_to_all(sent[-1], 'elem', split_axis=0, concat_axis=0, tiled=True)  7.88 us
    all_to_all x1, starting transfers between devices, shards(): lax.all_to_all(sent[-1], 'elem', split_axis=0, concat_axis=0, tiled=True)  7.3 us
    all_gather x1, blocking collectives, shards(): every = lax.all_gather(mine, 'snap', axis=0)  6.65 us
    all_gather x1, blocking collectives, shards(): coords = lax.all_gather(reduced_coords.T, 'snap', axis=0, tiled=True)  5.19 us
    pallas_call x1, Pallas kernels, shards(): pl.pallas_call(functools.partial(owner_kernel, devices, groups, capacity,...  3.29 us
  transfers between devices with their start and end apart: 1, of which 1 were waited for; matrix products, arithmetic and copies ran while one was open for 0% of the time, Pallas kernels for 1%

profile of v4, /device:TPU:0, one launch (start us, length us, event | category | flops | bytes accessed | tf_op | source)
XLA Modules:
  0.0 53.8 jit_solution(13884723889701741935)
XLA Ops:
  0.6 0.0 copy-start.2
  0.6 0.0 copy-start
  0.7 0.0 copy-start.3
  0.7 3.3 %owner_rows.1 = (bf16[8,64,512]{2,1,0:T(8,128)(2,1)}, f32[8,64]{1,0:T(8,128)}) custom-call(s32[1,64]{1,0:T(1,128)} %bitcast.12, s32[8,256]{1,0:T(8,128)} %bitcast.10, s32[64,128]{1,0:T(8,128)} %bitcast.9, s32[1,64]{1,0:T(1,128)} %bitcast.7, bf16[1024,1536]{1,0:T(8,128)(2,1)} %refs_4_.1), custom_call_target="tpu_custom_call" | custom-call | tf_op jit(solution)/shard_map/owner_rows/pallas_call | solution.py:501
  4.0 7.3 %all-to-all-start = ((bf16[8,64,512]{2,1,0:T(8,128)(2,1)}), bf16[8,64,512]{2,1,0:T(8,128)(2,1)S(1)}, u32[]{:S(2)}, u32[]{:S(2)}) async-start(bf16[8,64,512]{2,1,0:T(8,128)(2,1)} %get-tuple-element.8), calls=%async_computation | async-start | bytes 1048576 | tf_op jit(solution)/shard_map/all_to_all | solution.py:510
  11.3 0.0 copy-done.2
  11.3 0.0 copy-done
  11.3 0.0 copy-start.1
  11.3 0.7 %copy-done.1 = f32[8,64]{1,0:T(8,128)S(1)} copy-done((f32[8,64]{1,0:T(8,128)S(1)}, f32[8,64]{1,0:T(8,128)}, u32[]{:S(2)}) %copy-start.1) | copy-done | bytes 2072
  12.0 0.7 %place_tables.1 = (s32[1,512,128]{2,1,0:T(8,128)S(1)}, s32[512,128]{1,0:T(8,128)S(1)}, s32[512,128]{1,0:T(8,128)S(1)}, bf16[16,256,256]{2,1,0:T(8,128)(2,1)S(1)}) custom-call(f32[8,64]{1,0:T(8,128)S(1)} %copy-done.1, s32[1,64]{1,0:T(1,128)S(1)} %bitcast.8, bf16[16,24,24]{2,1,0:T(8,128)(2,1)S(1)} %copy-done), custom_call_target="tpu_custom_call" | custom-call | tf_op jit(solution)/shard_map/place_tables/pallas_call | solution.py:521
  12.7 0.0 copy-done.3
  12.7 5.2 %all_gather.9.coords = bf16[32,512]{1,0:T(8,128)(2,1)S(1)} all-gather(bf16[8,512]{1,0:T(8,128)(2,1)S(1)} %bitcast.11), channel_id=1, replica_groups=mesh['elem'=8,'snap'=4] {'snap'}, dimensions={0}, use_global_device_ids=true | all-gather | bytes 40960 | tf_op jit(solution)/shard_map/all_gather | solution.py:488
  17.9 7.9 %all-to-all-done.got = bf16[8,64,512]{2,1,0:T(8,128)(2,1)S(1)} async-done(((bf16[8,64,512]{2,1,0:T(8,128)(2,1)}), bf16[8,64,512]{2,1,0:T(8,128)(2,1)S(1)}, u32[]{:S(2)}, u32[]{:S(2)}) %all-to-all-start) | async-done | bytes 524320 | tf_op jit(solution)/shard_map/all_to_all | solution.py:510
  25.7 0.8 %element_squares.1 = bf16[96,512]{1,0:T(8,128)(2,1)S(1)} custom-call(bf16[8,64,512]{2,1,0:T(8,128)(2,1)S(1)} %all-to-all-done.got, bf16[32,512]{1,0:T(8,128)(2,1)S(1)} %all_gather.9.coords, s32[1,512,128]{2,1,0:T(8,128)S(1)} %get-tuple-element.10.places), custom_call_target="tpu_custom_call" | custom-call | tf_op jit(solution)/shard_map/element_squares/pallas_call | solution.py:529
  26.6 6.6 %all-gather = bf16[384,512]{1,0:T(8,128)(2,1)S(1)} all-gather(bf16[96,512]{1,0:T(8,128)(2,1)S(1)} %element_squares.1), channel_id=2, replica_groups=mesh['elem'=8,'snap'=4] {'snap'}, dimensions={0}, use_global_device_ids=true | all-gather | bytes 491520 | tf_op jit(solution)/shard_map/all_gather | solution.py:537
  33.2 20.4 %panel.1 = (f32[16,128,512]{2,1,0:T(8,128)}, f32[64,512]{1,0:T(8,128)}) custom-call(bf16[4,96,512]{2,1,0:T(8,128)(2,1)S(1)} %bitcast.6, bf16[8,64,512]{2,1,0:T(8,128)(2,1)S(1)} %all-to-all-done.got, s32[512,128]{1,0:T(8,128)S(1)} %get-tuple-element.11.places, s32[512,128]{1,0:T(8,128)S(1)} %get-tuple-element.12.slot_lane, ...), custom_call_target="tpu_custom_call" | custom-call | tf_op jit(solution)/shard_map/panel/pallas_call | solution.py:539
Async XLA Ops:
  0.6 10.6 %copy-start.2 = (s32[64]{0:T(128)S(1)}, s32[64]{0:T(128)}, u32[]{:S(2)}) copy-start(s32[64]{0:T(128)} %param.13) | copy-start | bytes 772
  0.6 10.6 %copy-start = (bf16[16,24,24]{2,1,0:T(8,128)(2,1)S(1)}, bf16[16,24,24]{2,1,0:T(8,128)(2,1)}, u32[]{:S(2)}) copy-start(bf16[16,24,24]{2,1,0:T(8,128)(2,1)} %stiff.1) | copy-start | bytes 55300
  0.7 12.0 %copy-start.3 = (bf16[512,8]{0,1:T(8,128)(2,1)S(1)}, bf16[512,8]{0,1:T(8,128)(2,1)}, u32[]{:S(2)}) copy-start(bf16[512,8]{0,1:T(8,128)(2,1)} %param.9) | copy-start | bytes 24580
  4.0 21.8 %all-to-all-start = ((bf16[8,64,512]{2,1,0:T(8,128)(2,1)}), bf16[8,64,512]{2,1,0:T(8,128)(2,1)S(1)}, u32[]{:S(2)}, u32[]{:S(2)}) async-start(bf16[8,64,512]{2,1,0:T(8,128)(2,1)} %get-tuple-element.8), calls=%async_computation | async-start | bytes 1048576 | tf_op jit(solution)/shard_map/all_to_all | solution.py:510
  11.3 0.7 %copy-start.1 = (f32[8,64]{1,0:T(8,128)S(1)}, f32[8,64]{1,0:T(8,128)}, u32[]{:S(2)}) copy-start(f32[8,64]{1,0:T(8,128)} %get-tuple-element.9.owners) | copy-start | bytes 6148

commit v5 on v4

--- a/solution.py
+++ b/solution.py
@@ -14,7 +14,7 @@
 LANES = 128
 TILE = 256
 BLOCK = 128
-PANEL = 64
+PANEL = 32
 STEP = 8
 MEBI = 1 << 20
 JOINED_LIMIT = 1 << 22

time: 54.1 us -> 54.1 us (level)
  no operation moved by 1% of the time
where the time goes in v5:
time: 54.1 us; the launch traced here: 53.8 us
  Pallas kernels  25.2 us (47%)
  blocking collectives  11.8 us (22%)
  waiting for transfers between devices  7.88 us (15%)
  starting transfers between devices  7.3 us (13%)
  between operations  0.89 us (2%)
  local copies, waits for them, and re-layouts  0.69 us (1%)
    pallas_call x1, Pallas kernels, shards(): pl.pallas_call(functools.partial(panel_kernel, ndof, pitch, total_rows),...  20.4 us
    all_to_all x1, waiting for transfers between devices, shards(): lax.all_to_all(sent[-1], 'elem', split_axis=0, concat_axis=0, tiled=True)  7.88 us
    all_to_all x1, starting transfers between devices, shards(): lax.all_to_all(sent[-1], 'elem', split_axis=0, concat_axis=0, tiled=True)  7.3 us
    all_gather x1, blocking collectives, shards(): every = lax.all_gather(mine, 'snap', axis=0)  6.65 us
    all_gather x1, blocking collectives, shards(): coords = lax.all_gather(reduced_coords.T, 'snap', axis=0, tiled=True)  5.19 us
    pallas_call x1, Pallas kernels, shards(): pl.pallas_call(functools.partial(owner_kernel, devices, groups, capacity,...  3.29 us
  transfers between devices with their start and end apart: 1, of which 1 were waited for; matrix products, arithmetic and copies ran while one was open for 0% of the time, Pallas kernels for 1%

profile of v5, /device:TPU:0, one launch (start us, length us, event | category | flops | bytes accessed | tf_op | source)
XLA Modules:
  0.0 53.8 jit_solution(14963379373549768848)
XLA Ops:
  0.6 0.0 copy-start.2
  0.6 0.0 copy-start
  0.7 0.0 copy-start.3
  0.7 3.3 %owner_rows.1 = (bf16[8,64,512]{2,1,0:T(8,128)(2,1)}, f32[8,64]{1,0:T(8,128)}) custom-call(s32[1,64]{1,0:T(1,128)} %bitcast.12, s32[8,256]{1,0:T(8,128)} %bitcast.10, s32[64,128]{1,0:T(8,128)} %bitcast.9, s32[1,64]{1,0:T(1,128)} %bitcast.7, bf16[1024,1536]{1,0:T(8,128)(2,1)} %refs_4_.1), custom_call_target="tpu_custom_call" | custom-call | tf_op jit(solution)/shard_map/owner_rows/pallas_call | solution.py:501
  4.0 7.3 %all-to-all-start = ((bf16[8,64,512]{2,1,0:T(8,128)(2,1)}), bf16[8,64,512]{2,1,0:T(8,128)(2,1)S(1)}, u32[]{:S(2)}, u32[]{:S(2)}) async-start(bf16[8,64,512]{2,1,0:T(8,128)(2,1)} %get-tuple-element.8), calls=%async_computation | async-start | bytes 1048576 | tf_op jit(solution)/shard_map/all_to_all | solution.py:510
  11.3 0.0 copy-done.2
  11.3 0.0 copy-done
  11.3 0.0 copy-start.1
  11.3 0.7 %copy-done.1 = f32[8,64]{1,0:T(8,128)S(1)} copy-done((f32[8,64]{1,0:T(8,128)S(1)}, f32[8,64]{1,0:T(8,128)}, u32[]{:S(2)}) %copy-start.1) | copy-done | bytes 2072
  12.0 0.7 %place_tables.1 = (s32[1,512,128]{2,1,0:T(8,128)S(1)}, s32[512,128]{1,0:T(8,128)S(1)}, s32[512,128]{1,0:T(8,128)S(1)}, bf16[16,256,256]{2,1,0:T(8,128)(2,1)S(1)}) custom-call(f32[8,64]{1,0:T(8,128)S(1)} %copy-done.1, s32[1,64]{1,0:T(1,128)S(1)} %bitcast.8, bf16[16,24,24]{2,1,0:T(8,128)(2,1)S(1)} %copy-done), custom_call_target="tpu_custom_call" | custom-call | tf_op jit(solution)/shard_map/place_tables/pallas_call | solution.py:521
  12.7 0.0 copy-done.3
  12.7 5.2 %all_gather.9.coords = bf16[32,512]{1,0:T(8,128)(2,1)S(1)} all-gather(bf16[8,512]{1,0:T(8,128)(2,1)S(1)} %bitcast.11), channel_id=1, replica_groups=mesh['elem'=8,'snap'=4] {'snap'}, dimensions={0}, use_global_device_ids=true | all-gather | bytes 40960 | tf_op jit(solution)/shard_map/all_gather | solution.py:488
  17.9 7.9 %all-to-all-done.got = bf16[8,64,512]{2,1,0:T(8,128)(2,1)S(1)} async-done(((bf16[8,64,512]{2,1,0:T(8,128)(2,1)}), bf16[8,64,512]{2,1,0:T(8,128)(2,1)S(1)}, u32[]{:S(2)}, u32[]{:S(2)}) %all-to-all-start) | async-done | bytes 524320 | tf_op jit(solution)/shard_map/all_to_all | solution.py:510
  25.7 0.8 %element_squares.1 = bf16[96,512]{1,0:T(8,128)(2,1)S(1)} custom-call(bf16[8,64,512]{2,1,0:T(8,128)(2,1)S(1)} %all-to-all-done.got, bf16[32,512]{1,0:T(8,128)(2,1)S(1)} %all_gather.9.coords, s32[1,512,128]{2,1,0:T(8,128)S(1)} %get-tuple-element.10.places), custom_call_target="tpu_custom_call" | custom-call | tf_op jit(solution)/shard_map/element_squares/pallas_call | solution.py:529
  26.6 6.6 %all-gather = bf16[384,512]{1,0:T(8,128)(2,1)S(1)} all-gather(bf16[96,512]{1,0:T(8,128)(2,1)S(1)} %element_squares.1), channel_id=2, replica_groups=mesh['elem'=8,'snap'=4] {'snap'}, dimensions={0}, use_global_device_ids=true | all-gather | bytes 491520 | tf_op jit(solution)/shard_map/all_gather | solution.py:537
  33.2 20.4 %panel.1 = (f32[16,128,512]{2,1,0:T(8,128)}, f32[64,512]{1,0:T(8,128)}) custom-call(bf16[4,96,512]{2,1,0:T(8,128)(2,1)S(1)} %bitcast.6, bf16[8,64,512]{2,1,0:T(8,128)(2,1)S(1)} %all-to-all-done.got, s32[512,128]{1,0:T(8,128)S(1)} %get-tuple-element.11.places, s32[512,128]{1,0:T(8,128)S(1)} %get-tuple-element.12.slot_lane, ...), custom_call_target="tpu_custom_call" | custom-call | tf_op jit(solution)/shard_map/panel/pallas_call | solution.py:539
Async XLA Ops:
  0.6 10.6 %copy-start.2 = (s32[64]{0:T(128)S(1)}, s32[64]{0:T(128)}, u32[]{:S(2)}) copy-start(s32[64]{0:T(128)} %param.13) | copy-start | bytes 772
  0.6 10.6 %copy-start = (bf16[16,24,24]{2,1,0:T(8,128)(2,1)S(1)}, bf16[16,24,24]{2,1,0:T(8,128)(2,1)}, u32[]{:S(2)}) copy-start(bf16[16,24,24]{2,1,0:T(8,128)(2,1)} %stiff.1) | copy-start | bytes 55300
  0.7 12.0 %copy-start.3 = (bf16[512,8]{0,1:T(8,128)(2,1)S(1)}, bf16[512,8]{0,1:T(8,128)(2,1)}, u32[]{:S(2)}) copy-start(bf16[512,8]{0,1:T(8,128)(2,1)} %param.9) | copy-start | bytes 24580
  4.0 21.8 %all-to-all-start = ((bf16[8,64,512]{2,1,0:T(8,128)(2,1)}), bf16[8,64,512]{2,1,0:T(8,128)(2,1)S(1)}, u32[]{:S(2)}, u32[]{:S(2)}) async-start(bf16[8,64,512]{2,1,0:T(8,128)(2,1)} %get-tuple-element.8), calls=%async_computation | async-start | bytes 1048576 | tf_op jit(solution)/shard_map/all_to_all | solution.py:510
  11.3 0.7 %copy-start.1 = (f32[8,64]{1,0:T(8,128)S(1)}, f32[8,64]{1,0:T(8,128)}, u32[]{:S(2)}) copy-start(f32[8,64]{1,0:T(8,128)} %get-tuple-element.9.owners) | copy-start | bytes 6148
